TPU v7x, 256 devices: a whole 4x4x8 slice. The times are simulated.
256 devices in a mesh: probe: 2 (over x_hi), gx: 16 (over z, core), gy: 8 (over y, x_lo).
Axes of the slice: x: 4 (x_hi: 2, x_lo: 2; x = x_hi * 2 + x_lo), y: 4, z: 8, core: 2. Of those that a mesh axis runs over, the one named last changes fastest.
Arguments:
- probes: float32 [8, 1024, 1024], P('probe', 'gx', 'gy'), may hold values from -6 to 6
- base_velocity: float32 [2, 1024, 1024], P(None, 'gx', 'gy'), may hold values from -6 to 6
- viscosity: float32 [1024, 1024], P('gx', 'gy'), may hold values from 0.1 to 0.4
- friction: float32 [1024, 1024], P('gx', 'gy'), may hold values from 0.25 to 1
- noise_weight: float32 [1024, 1024], P('gx', 'gy'), may hold values from 1 to 16
- ice_mask: int32 [1024, 1024], P('gx', 'gy'), may hold values 0 or 1
Outputs:
- images: float32 [8, 1024, 1024], P('probe', 'gx', 'gy')
- factor: float32 [8, 1024, 1024], P('probe', 'gx', 'gy')
- gram: float32 [8, 8], replicated
All inputs are finite; a program needn't handle non-finite values. No bound on the sum of `ice_mask` on one device may be relied on, other than what follows from the above.
Results may differ from a plain program's by a relative error of at most 0.000082.
Values sent between devices are 32-bit elements; how exact they have to be, the bound alone decides.
A program may use at most 64 MiB of HBM per device.

v0:
```python
import jax
import jax.numpy as jnp
from jax import lax
from jax.sharding import PartitionSpec as P

SWEEPS = 9


OMEGA = 0.6
DRAG = 0.05
PRIOR = 0.05


def extended(x, sides, width):
    for axis, dim in sides:
        size, length = (lax.axis_size(axis), x.shape[dim])
        up = [(i, (i + 1) % size) for i in range(size - 1)]
        down = [(j, i) for i, j in up]
        last = lax.slice_in_dim(x, length - width, length, axis=dim)
        first = lax.slice_in_dim(x, 0, width, axis=dim)
        before = lax.ppermute(last, axis, up)
        after = lax.ppermute(first, axis, down)
        x = jnp.concatenate([before, x, after], axis=dim)
    return x


def near(values, step_x, step_y):
    row_count = values.shape[-2]
    column_count = values.shape[-1]
    return values[..., 1 + step_x : row_count - 1 + step_x, 1 + step_y : column_count - 1 + step_y]


def diagonal_of(eta_pad, react):
    eta_mid = near(eta_pad, 0, 0)
    sum_first = near(eta_pad, 1, 0) + near(eta_pad, -1, 0)
    sum_second = near(eta_pad, 0, 1) + near(eta_pad, 0, -1)
    first = 2.0 * (2.0 * eta_mid + sum_first) + 0.5 * (2.0 * eta_mid + sum_second) + react
    second = 0.5 * (2.0 * eta_mid + sum_first) + 2.0 * (2.0 * eta_mid + sum_second) + react
    return jnp.stack([first, second], axis=-3)


def stencil(field_pad, eta_pad, react):
    eta_mid = near(eta_pad, 0, 0)
    eta_east = near(eta_pad, 1, 0)
    eta_west = near(eta_pad, -1, 0)
    eta_north = near(eta_pad, 0, 1)
    eta_south = near(eta_pad, 0, -1)
    along_x = field_pad[..., 0, :, :]
    along_y = field_pad[..., 1, :, :]
    x_mid = near(along_x, 0, 0)
    x_east = near(along_x, 1, 0)
    x_west = near(along_x, -1, 0)
    x_north = near(along_x, 0, 1)
    x_south = near(along_x, 0, -1)
    x_northeast = near(along_x, 1, 1)
    x_southeast = near(along_x, 1, -1)
    x_northwest = near(along_x, -1, 1)
    x_southwest = near(along_x, -1, -1)
    y_mid = near(along_y, 0, 0)
    y_east = near(along_y, 1, 0)
    y_west = near(along_y, -1, 0)
    y_north = near(along_y, 0, 1)
    y_south = near(along_y, 0, -1)
    y_northeast = near(along_y, 1, 1)
    y_southeast = near(along_y, 1, -1)
    y_northwest = near(along_y, -1, 1)
    y_southwest = near(along_y, -1, -1)
    first = (
        2.0 * (eta_mid + eta_east) * (x_mid - x_east)
        + 2.0 * (eta_mid + eta_west) * (x_mid - x_west)
        + 0.5 * (eta_mid + eta_north) * (x_mid - x_north)
        + 0.5 * (eta_mid + eta_south) * (x_mid - x_south)
        - 0.5 * (eta_east * (y_northeast - y_southeast) - eta_west * (y_northwest - y_southwest))
        - 0.25 * (eta_north * (y_northeast - y_northwest) - eta_south * (y_southeast - y_southwest))
        + react * x_mid
    )
    second = (
        0.5 * (eta_mid + eta_east) * (y_mid - y_east)
        + 0.5 * (eta_mid + eta_west) * (y_mid - y_west)
        + 2.0 * (eta_mid + eta_north) * (y_mid - y_north)
        + 2.0 * (eta_mid + eta_south) * (y_mid - y_south)
        - 0.5 * (eta_north * (x_northeast - x_northwest) - eta_south * (x_southeast - x_southwest))
        - 0.25 * (eta_east * (x_northeast - x_southeast) - eta_west * (x_northwest - x_southwest))
        + react * y_mid
    )
    return jnp.stack([first, second], axis=-3)


def body(probes, base_velocity, viscosity, friction, noise_weight, ice_mask):
    ice = ice_mask.astype(jnp.float32)
    coupling = friction * ice
    react = coupling + DRAG
    eta_pad = extended(viscosity, (("gx", 0), ("gy", 1)), 1)
    diag = diagonal_of(eta_pad, react)

    def relax(source):
        state = OMEGA * source / diag
        for sweep in range(SWEEPS - 1):
            padded = extended(state, (("gx", 2), ("gy", 3)), 1)
            state = state + OMEGA * (source - stencil(padded, eta_pad, react)) / diag
        return state

    source = (-coupling * base_velocity)[None] * probes[:, None]
    response = relax(source)
    adjoint = relax(noise_weight * response)
    images = -coupling * jnp.sum(base_velocity * adjoint, axis=1) + PRIOR * probes
    gathered = lax.all_gather(images, "probe", axis=0, tiled=True)
    probe_total = gathered.shape[0]
    flat_probes = probes.reshape(probes.shape[0], -1)
    flat_images = gathered.reshape(probe_total, -1)
    partial_rows = jnp.dot(flat_probes, flat_images.T, precision=lax.Precision.HIGHEST)
    total_cells = float(
        viscosity.shape[0] * lax.axis_size("gx") * viscosity.shape[1] * lax.axis_size("gy")
    )
    start = lax.axis_index("probe") * probes.shape[0]
    placed = lax.dynamic_update_slice(
        jnp.zeros((probe_total, probe_total), jnp.float32), partial_rows, (start, 0)
    )
    gram = lax.psum(placed, ("probe", "gx", "gy")) / total_cells
    lower = jnp.linalg.cholesky(gram)
    solved = jax.scipy.linalg.solve_triangular(lower, flat_images, lower=True)
    factor = lax.dynamic_slice_in_dim(solved, start, probes.shape[0], 0).reshape(probes.shape)
    return (images, factor, gram)


def solution(mesh):
    in_specs = (
        P("probe", "gx", "gy"),
        P(None, "gx", "gy"),
        P("gx", "gy"),
        P("gx", "gy"),
        P("gx", "gy"),
        P("gx", "gy"),
    )
    out_specs = (P("probe", "gx", "gy"), P("probe", "gx", "gy"), P())
    return jax.shard_map(body, mesh=mesh, in_specs=in_specs, out_specs=out_specs, check_vma=False)
```

profile of v0, /device:TPU:1, one launch (start us, length us, event | category | flops | bytes accessed | tf_op | source)
XLA Modules:
  0.0 494.4 jit_solution(14787006086745405829)
XLA Ops:
  1.3 5.1 %collective-permute-start = (f32[1,128]{1,0:T(1,128)S(1)}, f32[1,128]{1,0:T(1,128)S(1)}, u32[]{:S(2)}, u32[]{:S(2)}) collective-permute-start(f32[1,128]{1,0:T(1,128)S(1)} %get-tuple-element.130), channel_id=1, source_target_pairs={{8,0},{16,8},{24,16},{32,24},{40,32},{48,40},{56,48},{64,56},{72,6... | collective-permute-start | bytes 1544 | tf_op jit(solution)/shard_map/ppermute | solution.py:22
  11.7 4.0 collective-permute-start.3
  18.7 4.9 collective-permute-start.4
  25.5 3.0 collective-permute-done.5
  28.7 4.0 collective-permute-start.6
  34.0 4.1 collective-permute-done.6
  38.1 9.6 %collective-permute-done.7 = f32[4,2,66,1]{3,2,0,1:T(8,128)S(1)} collective-permute-done((f32[4,2,66,1]{3,2,0,1:T(8,128)S(1)}, f32[4,2,66,1]{3,2,0,1:T(8,128)S(1)}, u32[]{:S(2)}, u32[]{:S(2)}) %collective-permute-start.7) | collective-permute-done | bytes 2144 | tf_op jit(solution)/shard_map/ppermute | solution.py:22
  48.7 3.5 collective-permute-start.8
  54.1 3.0 collective-permute-done.9
  59.9 4.1 collective-permute-done.10
  64.0 9.8 %collective-permute-done.11 = f32[4,2,66,1]{3,2,0,1:T(8,128)S(1)} collective-permute-done((f32[4,2,66,1]{3,2,0,1:T(8,128)S(1)}, f32[4,2,66,1]{3,2,0,1:T(8,128)S(1)}, u32[]{:S(2)}, u32[]{:S(2)}) %collective-permute-start.11) | collective-permute-done | bytes 2144 | tf_op jit(solution)/shard_map/ppermute | solution.py:22
  75.0 3.7 collective-permute-start.12
  80.6 3.0 collective-permute-done.13
  86.4 4.1 collective-permute-done.14
  90.5 9.8 %collective-permute-done.15 = f32[4,2,66,1]{3,2,0,1:T(8,128)S(1)} collective-permute-done((f32[4,2,66,1]{3,2,0,1:T(8,128)S(1)}, f32[4,2,66,1]{3,2,0,1:T(8,128)S(1)}, u32[]{:S(2)}, u32[]{:S(2)}) %collective-permute-start.15) | collective-permute-done | bytes 2144 | tf_op jit(solution)/shard_map/ppermute | solution.py:22
  101.4 4.5 collective-permute-start.16
  107.9 3.0 collective-permute-done.17
  113.6 4.0 collective-permute-done.18
  117.6 6.5 %collective-permute-done.19 = f32[4,2,66,1]{3,2,0,1:T(8,128)S(1)} collective-permute-done((f32[4,2,66,1]{3,2,0,1:T(8,128)S(1)}, f32[4,2,66,1]{3,2,0,1:T(8,128)S(1)}, u32[]{:S(2)}, u32[]{:S(2)}) %collective-permute-start.19) | collective-permute-done | bytes 2144 | tf_op jit(solution)/shard_map/ppermute | solution.py:22
  130.1 3.0 collective-permute-done.21
  136.6 4.1 collective-permute-done.22
  140.7 6.5 %collective-permute-done.23 = f32[4,2,66,1]{3,2,0,1:T(8,128)S(1)} collective-permute-done((f32[4,2,66,1]{3,2,0,1:T(8,128)S(1)}, f32[4,2,66,1]{3,2,0,1:T(8,128)S(1)}, u32[]{:S(2)}, u32[]{:S(2)}) %collective-permute-start.23) | collective-permute-done | bytes 2144 | tf_op jit(solution)/shard_map/ppermute | solution.py:22
  148.4 4.2 collective-permute-start.24
  154.5 3.0 collective-permute-done.25
  161.0 4.1 collective-permute-done.26
  165.1 6.5 %collective-permute-done.27 = f32[4,2,66,1]{3,2,0,1:T(8,128)S(1)} collective-permute-done((f32[4,2,66,1]{3,2,0,1:T(8,128)S(1)}, f32[4,2,66,1]{3,2,0,1:T(8,128)S(1)}, u32[]{:S(2)}, u32[]{:S(2)}) %collective-permute-start.27) | collective-permute-done | bytes 2144 | tf_op jit(solution)/shard_map/ppermute | solution.py:22
  172.8 4.1 collective-permute-start.28
  178.8 3.0 collective-permute-done.29
  185.5 3.9 collective-permute-done.30
  189.4 6.5 %collective-permute-done.31 = f32[4,2,66,1]{3,2,0,1:T(8,128)S(1)} collective-permute-done((f32[4,2,66,1]{3,2,0,1:T(8,128)S(1)}, f32[4,2,66,1]{3,2,0,1:T(8,128)S(1)}, u32[]{:S(2)}, u32[]{:S(2)}) %collective-permute-start.31) | collective-permute-done | bytes 2144 | tf_op jit(solution)/shard_map/ppermute | solution.py:22
  197.2 3.8 collective-permute-start.32
  202.9 3.0 collective-permute-done.33
  209.4 4.1 collective-permute-done.34
  213.5 6.5 %collective-permute-done.35 = f32[4,2,66,1]{3,2,0,1:T(8,128)S(1)} collective-permute-done((f32[4,2,66,1]{3,2,0,1:T(8,128)S(1)}, f32[4,2,66,1]{3,2,0,1:T(8,128)S(1)}, u32[]{:S(2)}, u32[]{:S(2)}) %collective-permute-start.35) | collective-permute-done | bytes 2144 | tf_op jit(solution)/shard_map/ppermute | solution.py:22
  221.8 3.4 collective-permute-start.36
  227.1 3.0 collective-permute-done.37
  233.6 4.1 collective-permute-done.38
  237.7 6.5 %collective-permute-done.39 = f32[4,2,66,1]{3,2,0,1:T(8,128)S(1)} collective-permute-done((f32[4,2,66,1]{3,2,0,1:T(8,128)S(1)}, f32[4,2,66,1]{3,2,0,1:T(8,128)S(1)}, u32[]{:S(2)}, u32[]{:S(2)}) %collective-permute-start.39) | collective-permute-done | bytes 2144 | tf_op jit(solution)/shard_map/ppermute | solution.py:22
  250.1 3.0 collective-permute-done.41
  256.6 4.1 collective-permute-done.42
  260.7 6.5 %collective-permute-done.43 = f32[4,2,66,1]{3,2,0,1:T(8,128)S(1)} collective-permute-done((f32[4,2,66,1]{3,2,0,1:T(8,128)S(1)}, f32[4,2,66,1]{3,2,0,1:T(8,128)S(1)}, u32[]{:S(2)}, u32[]{:S(2)}) %collective-permute-start.43) | collective-permute-done | bytes 2144 | tf_op jit(solution)/shard_map/ppermute | solution.py:22
  273.0 3.0 collective-permute-done.45
  279.4 4.1 collective-permute-done.46
  283.5 6.5 %collective-permute-done.47 = f32[4,2,66,1]{3,2,0,1:T(8,128)S(1)} collective-permute-done((f32[4,2,66,1]{3,2,0,1:T(8,128)S(1)}, f32[4,2,66,1]{3,2,0,1:T(8,128)S(1)}, u32[]{:S(2)}, u32[]{:S(2)}) %collective-permute-start.47) | collective-permute-done | bytes 2144 | tf_op jit(solution)/shard_map/ppermute | solution.py:22
  295.8 3.0 collective-permute-done.49
  302.3 4.1 collective-permute-done.50
  306.4 6.5 %collective-permute-done.51 = f32[4,2,66,1]{3,2,0,1:T(8,128)S(1)} collective-permute-done((f32[4,2,66,1]{3,2,0,1:T(8,128)S(1)}, f32[4,2,66,1]{3,2,0,1:T(8,128)S(1)}, u32[]{:S(2)}, u32[]{:S(2)}) %collective-permute-start.51) | collective-permute-done | bytes 2144 | tf_op jit(solution)/shard_map/ppermute | solution.py:22
  313.9 3.2 collective-permute-start.52
  319.1 3.0 collective-permute-done.53
  325.3 4.1 collective-permute-done.54
  329.4 6.5 %collective-permute-done.55 = f32[4,2,66,1]{3,2,0,1:T(8,128)S(1)} collective-permute-done((f32[4,2,66,1]{3,2,0,1:T(8,128)S(1)}, f32[4,2,66,1]{3,2,0,1:T(8,128)S(1)}, u32[]{:S(2)}, u32[]{:S(2)}) %collective-permute-start.55) | collective-permute-done | bytes 2144 | tf_op jit(solution)/shard_map/ppermute | solution.py:22
  336.9 3.8 collective-permute-start.56
  342.7 3.0 collective-permute-done.57
  349.4 3.9 collective-permute-done.58
  353.3 6.5 %collective-permute-done.59 = f32[4,2,66,1]{3,2,0,1:T(8,128)S(1)} collective-permute-done((f32[4,2,66,1]{3,2,0,1:T(8,128)S(1)}, f32[4,2,66,1]{3,2,0,1:T(8,128)S(1)}, u32[]{:S(2)}, u32[]{:S(2)}) %collective-permute-start.59) | collective-permute-done | bytes 2144 | tf_op jit(solution)/shard_map/ppermute | solution.py:22
  360.8 3.5 collective-permute-start.60
  366.3 3.0 collective-permute-done.61
  372.7 4.1 collective-permute-done.62
  376.8 6.5 %collective-permute-done.63 = f32[4,2,66,1]{3,2,0,1:T(8,128)S(1)} collective-permute-done((f32[4,2,66,1]{3,2,0,1:T(8,128)S(1)}, f32[4,2,66,1]{3,2,0,1:T(8,128)S(1)}, u32[]{:S(2)}, u32[]{:S(2)}) %collective-permute-start.63) | collective-permute-done | bytes 2144 | tf_op jit(solution)/shard_map/ppermute | solution.py:22
  389.2 3.0 collective-permute-done.65
  395.7 4.1 collective-permute-done.66
  399.8 6.5 %collective-permute-done.67 = f32[4,2,66,1]{3,2,1,0:T(8,128)S(1)} collective-permute-done((f32[4,2,66,1]{3,2,1,0:T(8,128)S(1)}, f32[4,2,66,1]{3,2,1,0:T(8,128)S(1)}, u32[]{:S(2)}, u32[]{:S(2)}) %collective-permute-start.67) | collective-permute-done | bytes 2144 | tf_op jit(solution)/shard_map/ppermute | solution.py:22
  407.4 6.8 %all_gather.3 = f32[8,64,128]{2,1,0:T(8,128)S(1)} all-gather(f32[4,64,128]{2,1,0:T(8,128)S(1)} %multiply_add_fusion), channel_id=1, replica_groups=mesh['probe'=2,'gx'=16,'gy'=8] {'probe'}, dimensions={0}, use_global_device_ids=true | all-gather | bytes 393216 | tf_op jit(solution)/shard_map/all_gather | solution.py:107
  415.1 74.6 %psum.7 = f32[8,8]{0,1:T(8,128)S(1)} all-reduce(f32[8,8]{0,1:T(8,128)S(1)} %dynamic_update_slice.3), channel_id=1, replica_groups=mesh['probe'=2,'gx'=16,'gy'=8] {'probe','gx','gy'}, use_global_device_ids=true, to_apply=%region_1.0 | all-reduce | flops 64 | bytes 512 | tf_op jit(solution)/shard_map/psum | solution.py:119
  (243 shorter events, 128.7 us)
Async XLA Ops:
  1.3 7.1 %collective-permute-start = (f32[1,128]{1,0:T(1,128)S(1)}, f32[1,128]{1,0:T(1,128)S(1)}, u32[]{:S(2)}, u32[]{:S(2)}) collective-permute-start(f32[1,128]{1,0:T(1,128)S(1)} %get-tuple-element.130), channel_id=1, source_target_pairs={{8,0},{16,8},{24,16},{32,24},{40,32},{48,40},{56,48},{64,56},{72,6... | collective-permute-start | bytes 1544 | tf_op jit(solution)/shard_map/ppermute | solution.py:22
  10.3 5.3 %collective-permute-start.2 = (f32[66,1]{1,0:T(8,128)S(1)}, f32[66,1]{1,0:T(8,128)S(1)}, u32[]{:S(2)}, u32[]{:S(2)}) collective-permute-start(f32[66,1]{1,0:T(8,128)S(1)} %get-tuple-element.121), channel_id=1, source_target_pairs={{1,0},{2,1},{3,2},{4,3},{5,4},{6,5},{7,6},{9,8},{10,9},{11,10},{12... | collective-permute-start | bytes 800 | tf_op jit(solution)/shard_map/ppermute | solution.py:22
  11.7 5.0 %collective-permute-start.3 = (f32[66,1]{1,0:T(8,128)S(1)}, f32[66,1]{1,0:T(8,128)S(1)}, u32[]{:S(2)}, u32[]{:S(2)}) collective-permute-start(f32[66,1]{1,0:T(8,128)S(1)} %get-tuple-element.120), channel_id=1, source_target_pairs={{0,1},{1,2},{2,3},{3,4},{4,5},{5,6},{6,7},{8,9},{9,10},{10,11},{11... | collective-permute-start | bytes 800 | tf_op jit(solution)/shard_map/ppermute | solution.py:21
  18.7 6.8 %collective-permute-start.4 = (f32[4,2,1,128]{3,2,0,1:T(1,128)S(1)}, f32[4,2,1,128]{3,2,0,1:T(1,128)S(1)}, u32[]{:S(2)}, u32[]{:S(2)}) collective-permute-start(f32[4,2,1,128]{3,2,0,1:T(1,128)S(1)} %get-tuple-element.114), channel_id=1, source_target_pairs={{0,8},{8,16},{16,24},{24,32},{32,40},{40,48},{48,56},{56,64},{64,7... | collective-permute-start | bytes 12296 | tf_op jit(solution)/shard_map/ppermute | solution.py:21
  23.6 4.9 collective-permute-start.5
  28.7 9.4 %collective-permute-start.6 = (f32[4,2,66,1]{3,2,0,1:T(8,128)S(1)}, f32[4,2,66,1]{3,2,0,1:T(8,128)S(1)}, u32[]{:S(2)}, u32[]{:S(2)}) collective-permute-start(f32[4,2,66,1]{3,2,0,1:T(8,128)S(1)} %get-tuple-element.82), channel_id=1, source_target_pairs={{0,1},{1,2},{2,3},{3,4},{4,5},{5,6},{6,7},{8,9},{9,10},{10,11},{11... | collective-permute-start | bytes 6344 | tf_op jit(solution)/shard_map/ppermute | solution.py:21
  32.7 15.0 %collective-permute-start.7 = (f32[4,2,66,1]{3,2,0,1:T(8,128)S(1)}, f32[4,2,66,1]{3,2,0,1:T(8,128)S(1)}, u32[]{:S(2)}, u32[]{:S(2)}) collective-permute-start(f32[4,2,66,1]{3,2,0,1:T(8,128)S(1)} %get-tuple-element.83), channel_id=1, source_target_pairs={{1,0},{2,1},{3,2},{4,3},{5,4},{6,5},{7,6},{9,8},{10,9},{11,10},{12... | collective-permute-start | bytes 6344 | tf_op jit(solution)/shard_map/ppermute | solution.py:22
  48.7 5.4 %collective-permute-start.8 = (f32[4,2,1,128]{3,2,0,1:T(1,128)S(1)}, f32[4,2,1,128]{3,2,0,1:T(1,128)S(1)}, u32[]{:S(2)}, u32[]{:S(2)}) collective-permute-start(f32[4,2,1,128]{3,2,0,1:T(1,128)S(1)} %get-tuple-element.112), channel_id=1, source_target_pairs={{0,8},{8,16},{16,24},{24,32},{32,40},{40,48},{48,56},{56,64},{64,7... | collective-permute-start | bytes 12296 | tf_op jit(solution)/shard_map/ppermute | solution.py:21
  52.2 4.9 collective-permute-start.9
  57.3 6.7 %collective-permute-start.10 = (f32[4,2,66,1]{3,2,0,1:T(8,128)S(1)}, f32[4,2,66,1]{3,2,0,1:T(8,128)S(1)}, u32[]{:S(2)}, u32[]{:S(2)}) collective-permute-start(f32[4,2,66,1]{3,2,0,1:T(8,128)S(1)} %get-tuple-element.80), channel_id=1, source_target_pairs={{0,1},{1,2},{2,3},{3,4},{4,5},{5,6},{6,7},{8,9},{9,10},{10,11},{11... | collective-permute-start | bytes 6344 | tf_op jit(solution)/shard_map/ppermute | solution.py:21
  58.6 15.2 %collective-permute-start.11 = (f32[4,2,66,1]{3,2,0,1:T(8,128)S(1)}, f32[4,2,66,1]{3,2,0,1:T(8,128)S(1)}, u32[]{:S(2)}, u32[]{:S(2)}) collective-permute-start(f32[4,2,66,1]{3,2,0,1:T(8,128)S(1)} %get-tuple-element.81), channel_id=1, source_target_pairs={{1,0},{2,1},{3,2},{4,3},{5,4},{6,5},{7,6},{9,8},{10,9},{11,10},{12... | collective-permute-start | bytes 6344 | tf_op jit(solution)/shard_map/ppermute | solution.py:22
  75.0 5.6 %collective-permute-start.12 = (f32[4,2,1,128]{3,2,0,1:T(1,128)S(1)}, f32[4,2,1,128]{3,2,0,1:T(1,128)S(1)}, u32[]{:S(2)}, u32[]{:S(2)}) collective-permute-start(f32[4,2,1,128]{3,2,0,1:T(1,128)S(1)} %get-tuple-element.110), channel_id=1, source_target_pairs={{0,8},{8,16},{16,24},{24,32},{32,40},{40,48},{48,56},{56,64},{64,7... | collective-permute-start | bytes 12296 | tf_op jit(solution)/shard_map/ppermute | solution.py:21
  78.6 4.9 collective-permute-start.13
  83.7 6.7 %collective-permute-start.14 = (f32[4,2,66,1]{3,2,0,1:T(8,128)S(1)}, f32[4,2,66,1]{3,2,0,1:T(8,128)S(1)}, u32[]{:S(2)}, u32[]{:S(2)}) collective-permute-start(f32[4,2,66,1]{3,2,0,1:T(8,128)S(1)} %get-tuple-element.78), channel_id=1, source_target_pairs={{0,1},{1,2},{2,3},{3,4},{4,5},{5,6},{6,7},{8,9},{9,10},{10,11},{11... | collective-permute-start | bytes 6344 | tf_op jit(solution)/shard_map/ppermute | solution.py:21
  85.1 15.2 %collective-permute-start.15 = (f32[4,2,66,1]{3,2,0,1:T(8,128)S(1)}, f32[4,2,66,1]{3,2,0,1:T(8,128)S(1)}, u32[]{:S(2)}, u32[]{:S(2)}) collective-permute-start(f32[4,2,66,1]{3,2,0,1:T(8,128)S(1)} %get-tuple-element.79), channel_id=1, source_target_pairs={{1,0},{2,1},{3,2},{4,3},{5,4},{6,5},{7,6},{9,8},{10,9},{11,10},{12... | collective-permute-start | bytes 6344 | tf_op jit(solution)/shard_map/ppermute | solution.py:22
  101.4 6.4 %collective-permute-start.16 = (f32[4,2,1,128]{3,2,0,1:T(1,128)S(1)}, f32[4,2,1,128]{3,2,0,1:T(1,128)S(1)}, u32[]{:S(2)}, u32[]{:S(2)}) collective-permute-start(f32[4,2,1,128]{3,2,0,1:T(1,128)S(1)} %get-tuple-element.108), channel_id=1, source_target_pairs={{0,8},{8,16},{16,24},{24,32},{32,40},{40,48},{48,56},{56,64},{64,7... | collective-permute-start | bytes 12296 | tf_op jit(solution)/shard_map/ppermute | solution.py:21
  105.9 4.9 collective-permute-start.17
  111.0 6.6 %collective-permute-start.18 = (f32[4,2,66,1]{3,2,0,1:T(8,128)S(1)}, f32[4,2,66,1]{3,2,0,1:T(8,128)S(1)}, u32[]{:S(2)}, u32[]{:S(2)}) collective-permute-start(f32[4,2,66,1]{3,2,0,1:T(8,128)S(1)} %get-tuple-element.76), channel_id=1, source_target_pairs={{0,1},{1,2},{2,3},{3,4},{4,5},{5,6},{6,7},{8,9},{9,10},{10,11},{11... | collective-permute-start | bytes 6344 | tf_op jit(solution)/shard_map/ppermute | solution.py:21
  112.3 11.8 %collective-permute-start.19 = (f32[4,2,66,1]{3,2,0,1:T(8,128)S(1)}, f32[4,2,66,1]{3,2,0,1:T(8,128)S(1)}, u32[]{:S(2)}, u32[]{:S(2)}) collective-permute-start(f32[4,2,66,1]{3,2,0,1:T(8,128)S(1)} %get-tuple-element.77), channel_id=1, source_target_pairs={{1,0},{2,1},{3,2},{4,3},{5,4},{6,5},{7,6},{9,8},{10,9},{11,10},{12... | collective-permute-start | bytes 6344 | tf_op jit(solution)/shard_map/ppermute | solution.py:22
  128.2 4.9 collective-permute-start.21
  133.3 7.4 %collective-permute-start.22 = (f32[4,2,66,1]{3,2,0,1:T(8,128)S(1)}, f32[4,2,66,1]{3,2,0,1:T(8,128)S(1)}, u32[]{:S(2)}, u32[]{:S(2)}) collective-permute-start(f32[4,2,66,1]{3,2,0,1:T(8,128)S(1)} %get-tuple-element.74), channel_id=1, source_target_pairs={{0,1},{1,2},{2,3},{3,4},{4,5},{5,6},{6,7},{8,9},{9,10},{10,11},{11... | collective-permute-start | bytes 6344 | tf_op jit(solution)/shard_map/ppermute | solution.py:21
  135.3 11.9 %collective-permute-start.23 = (f32[4,2,66,1]{3,2,0,1:T(8,128)S(1)}, f32[4,2,66,1]{3,2,0,1:T(8,128)S(1)}, u32[]{:S(2)}, u32[]{:S(2)}) collective-permute-start(f32[4,2,66,1]{3,2,0,1:T(8,128)S(1)} %get-tuple-element.75), channel_id=1, source_target_pairs={{1,0},{2,1},{3,2},{4,3},{5,4},{6,5},{7,6},{9,8},{10,9},{11,10},{12... | collective-permute-start | bytes 6344 | tf_op jit(solution)/shard_map/ppermute | solution.py:22
  148.4 6.1 %collective-permute-start.24 = (f32[4,2,1,128]{3,2,0,1:T(1,128)S(1)}, f32[4,2,1,128]{3,2,0,1:T(1,128)S(1)}, u32[]{:S(2)}, u32[]{:S(2)}) collective-permute-start(f32[4,2,1,128]{3,2,0,1:T(1,128)S(1)} %get-tuple-element.104), channel_id=1, source_target_pairs={{0,8},{8,16},{16,24},{24,32},{32,40},{40,48},{48,56},{56,64},{64,7... | collective-permute-start | bytes 12296 | tf_op jit(solution)/shard_map/ppermute | solution.py:21
  152.6 4.9 collective-permute-start.25
  157.7 7.4 %collective-permute-start.26 = (f32[4,2,66,1]{3,2,0,1:T(8,128)S(1)}, f32[4,2,66,1]{3,2,0,1:T(8,128)S(1)}, u32[]{:S(2)}, u32[]{:S(2)}) collective-permute-start(f32[4,2,66,1]{3,2,0,1:T(8,128)S(1)} %get-tuple-element.72), channel_id=1, source_target_pairs={{0,1},{1,2},{2,3},{3,4},{4,5},{5,6},{6,7},{8,9},{9,10},{10,11},{11... | collective-permute-start | bytes 6344 | tf_op jit(solution)/shard_map/ppermute | solution.py:21
  159.7 11.9 %collective-permute-start.27 = (f32[4,2,66,1]{3,2,0,1:T(8,128)S(1)}, f32[4,2,66,1]{3,2,0,1:T(8,128)S(1)}, u32[]{:S(2)}, u32[]{:S(2)}) collective-permute-start(f32[4,2,66,1]{3,2,0,1:T(8,128)S(1)} %get-tuple-element.73), channel_id=1, source_target_pairs={{1,0},{2,1},{3,2},{4,3},{5,4},{6,5},{7,6},{9,8},{10,9},{11,10},{12... | collective-permute-start | bytes 6344 | tf_op jit(solution)/shard_map/ppermute | solution.py:22
  172.8 6.0 %collective-permute-start.28 = (f32[4,2,1,128]{3,2,0,1:T(1,128)S(1)}, f32[4,2,1,128]{3,2,0,1:T(1,128)S(1)}, u32[]{:S(2)}, u32[]{:S(2)}) collective-permute-start(f32[4,2,1,128]{3,2,0,1:T(1,128)S(1)} %get-tuple-element.102), channel_id=1, source_target_pairs={{0,8},{8,16},{16,24},{24,32},{32,40},{40,48},{48,56},{56,64},{64,7... | collective-permute-start | bytes 12296 | tf_op jit(solution)/shard_map/ppermute | solution.py:21
  176.9 4.9 collective-permute-start.29
  182.0 7.4 %collective-permute-start.30 = (f32[4,2,66,1]{3,2,0,1:T(8,128)S(1)}, f32[4,2,66,1]{3,2,0,1:T(8,128)S(1)}, u32[]{:S(2)}, u32[]{:S(2)}) collective-permute-start(f32[4,2,66,1]{3,2,0,1:T(8,128)S(1)} %get-tuple-element.70), channel_id=1, source_target_pairs={{0,1},{1,2},{2,3},{3,4},{4,5},{5,6},{6,7},{8,9},{9,10},{10,11},{11... | collective-permute-start | bytes 6344 | tf_op jit(solution)/shard_map/ppermute | solution.py:21
  184.0 11.9 %collective-permute-start.31 = (f32[4,2,66,1]{3,2,0,1:T(8,128)S(1)}, f32[4,2,66,1]{3,2,0,1:T(8,128)S(1)}, u32[]{:S(2)}, u32[]{:S(2)}) collective-permute-start(f32[4,2,66,1]{3,2,0,1:T(8,128)S(1)} %get-tuple-element.71), channel_id=1, source_target_pairs={{1,0},{2,1},{3,2},{4,3},{5,4},{6,5},{7,6},{9,8},{10,9},{11,10},{12... | collective-permute-start | bytes 6344 | tf_op jit(solution)/shard_map/ppermute | solution.py:22
  197.2 5.8 %collective-permute-start.32 = (f32[4,2,1,128]{3,2,0,1:T(1,128)S(1)}, f32[4,2,1,128]{3,2,0,1:T(1,128)S(1)}, u32[]{:S(2)}, u32[]{:S(2)}) collective-permute-start(f32[4,2,1,128]{3,2,0,1:T(1,128)S(1)} %get-tuple-element.100), channel_id=1, source_target_pairs={{0,8},{8,16},{16,24},{24,32},{32,40},{40,48},{48,56},{56,64},{64,7... | collective-permute-start | bytes 12296 | tf_op jit(solution)/shard_map/ppermute | solution.py:21
  201.0 4.9 collective-permute-start.33
  206.1 7.4 %collective-permute-start.34 = (f32[4,2,66,1]{3,2,0,1:T(8,128)S(1)}, f32[4,2,66,1]{3,2,0,1:T(8,128)S(1)}, u32[]{:S(2)}, u32[]{:S(2)}) collective-permute-start(f32[4,2,66,1]{3,2,0,1:T(8,128)S(1)} %get-tuple-element.68), channel_id=1, source_target_pairs={{0,1},{1,2},{2,3},{3,4},{4,5},{5,6},{6,7},{8,9},{9,10},{10,11},{11... | collective-permute-start | bytes 6344 | tf_op jit(solution)/shard_map/ppermute | solution.py:21
  208.1 11.9 %collective-permute-start.35 = (f32[4,2,66,1]{3,2,0,1:T(8,128)S(1)}, f32[4,2,66,1]{3,2,0,1:T(8,128)S(1)}, u32[]{:S(2)}, u32[]{:S(2)}) collective-permute-start(f32[4,2,66,1]{3,2,0,1:T(8,128)S(1)} %get-tuple-element.69), channel_id=1, source_target_pairs={{1,0},{2,1},{3,2},{4,3},{5,4},{6,5},{7,6},{9,8},{10,9},{11,10},{12... | collective-permute-start | bytes 6344 | tf_op jit(solution)/shard_map/ppermute | solution.py:22
  221.8 5.4 %collective-permute-start.36 = (f32[4,2,1,128]{3,2,0,1:T(1,128)S(1)}, f32[4,2,1,128]{3,2,0,1:T(1,128)S(1)}, u32[]{:S(2)}, u32[]{:S(2)}) collective-permute-start(f32[4,2,1,128]{3,2,0,1:T(1,128)S(1)} %get-tuple-element.98), channel_id=1, source_target_pairs={{0,8},{8,16},{16,24},{24,32},{32,40},{40,48},{48,56},{56,64},{64,7... | collective-permute-start | bytes 12296 | tf_op jit(solution)/shard_map/ppermute | solution.py:21
  225.2 4.9 collective-permute-start.37
  230.3 7.4 %collective-permute-start.38 = (f32[4,2,66,1]{3,2,0,1:T(8,128)S(1)}, f32[4,2,66,1]{3,2,0,1:T(8,128)S(1)}, u32[]{:S(2)}, u32[]{:S(2)}) collective-permute-start(f32[4,2,66,1]{3,2,0,1:T(8,128)S(1)} %get-tuple-element.66), channel_id=1, source_target_pairs={{0,1},{1,2},{2,3},{3,4},{4,5},{5,6},{6,7},{8,9},{9,10},{10,11},{11... | collective-permute-start | bytes 6344 | tf_op jit(solution)/shard_map/ppermute | solution.py:21
  232.3 11.9 %collective-permute-start.39 = (f32[4,2,66,1]{3,2,0,1:T(8,128)S(1)}, f32[4,2,66,1]{3,2,0,1:T(8,128)S(1)}, u32[]{:S(2)}, u32[]{:S(2)}) collective-permute-start(f32[4,2,66,1]{3,2,0,1:T(8,128)S(1)} %get-tuple-element.67), channel_id=1, source_target_pairs={{1,0},{2,1},{3,2},{4,3},{5,4},{6,5},{7,6},{9,8},{10,9},{11,10},{12... | collective-permute-start | bytes 6344 | tf_op jit(solution)/shard_map/ppermute | solution.py:22
  245.2 4.9 collective-permute-start.40
  248.2 4.9 collective-permute-start.41
  253.3 7.4 %collective-permute-start.42 = (f32[4,2,66,1]{3,2,0,1:T(8,128)S(1)}, f32[4,2,66,1]{3,2,0,1:T(8,128)S(1)}, u32[]{:S(2)}, u32[]{:S(2)}) collective-permute-start(f32[4,2,66,1]{3,2,0,1:T(8,128)S(1)} %get-tuple-element.64), channel_id=1, source_target_pairs={{0,1},{1,2},{2,3},{3,4},{4,5},{5,6},{6,7},{8,9},{9,10},{10,11},{11... | collective-permute-start | bytes 6344 | tf_op jit(solution)/shard_map/ppermute | solution.py:21
  255.3 11.9 %collective-permute-start.43 = (f32[4,2,66,1]{3,2,0,1:T(8,128)S(1)}, f32[4,2,66,1]{3,2,0,1:T(8,128)S(1)}, u32[]{:S(2)}, u32[]{:S(2)}) collective-permute-start(f32[4,2,66,1]{3,2,0,1:T(8,128)S(1)} %get-tuple-element.65), channel_id=1, source_target_pairs={{1,0},{2,1},{3,2},{4,3},{5,4},{6,5},{7,6},{9,8},{10,9},{11,10},{12... | collective-permute-start | bytes 6344 | tf_op jit(solution)/shard_map/ppermute | solution.py:22
  271.0 4.9 collective-permute-start.45
  276.1 7.4 %collective-permute-start.46 = (f32[4,2,66,1]{3,2,0,1:T(8,128)S(1)}, f32[4,2,66,1]{3,2,0,1:T(8,128)S(1)}, u32[]{:S(2)}, u32[]{:S(2)}) collective-permute-start(f32[4,2,66,1]{3,2,0,1:T(8,128)S(1)} %get-tuple-element.62), channel_id=1, source_target_pairs={{0,1},{1,2},{2,3},{3,4},{4,5},{5,6},{6,7},{8,9},{9,10},{10,11},{11... | collective-permute-start | bytes 6344 | tf_op jit(solution)/shard_map/ppermute | solution.py:21
  278.1 11.9 %collective-permute-start.47 = (f32[4,2,66,1]{3,2,0,1:T(8,128)S(1)}, f32[4,2,66,1]{3,2,0,1:T(8,128)S(1)}, u32[]{:S(2)}, u32[]{:S(2)}) collective-permute-start(f32[4,2,66,1]{3,2,0,1:T(8,128)S(1)} %get-tuple-element.63), channel_id=1, source_target_pairs={{1,0},{2,1},{3,2},{4,3},{5,4},{6,5},{7,6},{9,8},{10,9},{11,10},{12... | collective-permute-start | bytes 6344 | tf_op jit(solution)/shard_map/ppermute | solution.py:22
  293.9 4.9 collective-permute-start.49
  299.0 7.4 %collective-permute-start.50 = (f32[4,2,66,1]{3,2,0,1:T(8,128)S(1)}, f32[4,2,66,1]{3,2,0,1:T(8,128)S(1)}, u32[]{:S(2)}, u32[]{:S(2)}) collective-permute-start(f32[4,2,66,1]{3,2,0,1:T(8,128)S(1)} %get-tuple-element.60), channel_id=1, source_target_pairs={{0,1},{1,2},{2,3},{3,4},{4,5},{5,6},{6,7},{8,9},{9,10},{10,11},{11... | collective-permute-start | bytes 6344 | tf_op jit(solution)/shard_map/ppermute | solution.py:21
  301.0 11.9 %collective-permute-start.51 = (f32[4,2,66,1]{3,2,0,1:T(8,128)S(1)}, f32[4,2,66,1]{3,2,0,1:T(8,128)S(1)}, u32[]{:S(2)}, u32[]{:S(2)}) collective-permute-start(f32[4,2,66,1]{3,2,0,1:T(8,128)S(1)} %get-tuple-element.61), channel_id=1, source_target_pairs={{1,0},{2,1},{3,2},{4,3},{5,4},{6,5},{7,6},{9,8},{10,9},{11,10},{12... | collective-permute-start | bytes 6344 | tf_op jit(solution)/shard_map/ppermute | solution.py:22
  313.9 5.1 %collective-permute-start.52 = (f32[4,2,1,128]{3,2,0,1:T(1,128)S(1)}, f32[4,2,1,128]{3,2,0,1:T(1,128)S(1)}, u32[]{:S(2)}, u32[]{:S(2)}) collective-permute-start(f32[4,2,1,128]{3,2,0,1:T(1,128)S(1)} %get-tuple-element.90), channel_id=1, source_target_pairs={{0,8},{8,16},{16,24},{24,32},{32,40},{40,48},{48,56},{56,64},{64,7... | collective-permute-start | bytes 12296 | tf_op jit(solution)/shard_map/ppermute | solution.py:21
  317.1 4.9 collective-permute-start.53
  322.2 7.2 %collective-permute-start.54 = (f32[4,2,66,1]{3,2,0,1:T(8,128)S(1)}, f32[4,2,66,1]{3,2,0,1:T(8,128)S(1)}, u32[]{:S(2)}, u32[]{:S(2)}) collective-permute-start(f32[4,2,66,1]{3,2,0,1:T(8,128)S(1)} %get-tuple-element.58), channel_id=1, source_target_pairs={{0,1},{1,2},{2,3},{3,4},{4,5},{5,6},{6,7},{8,9},{9,10},{10,11},{11... | collective-permute-start | bytes 6344 | tf_op jit(solution)/shard_map/ppermute | solution.py:21
  324.0 11.9 %collective-permute-start.55 = (f32[4,2,66,1]{3,2,0,1:T(8,128)S(1)}, f32[4,2,66,1]{3,2,0,1:T(8,128)S(1)}, u32[]{:S(2)}, u32[]{:S(2)}) collective-permute-start(f32[4,2,66,1]{3,2,0,1:T(8,128)S(1)} %get-tuple-element.59), channel_id=1, source_target_pairs={{1,0},{2,1},{3,2},{4,3},{5,4},{6,5},{7,6},{9,8},{10,9},{11,10},{12... | collective-permute-start | bytes 6344 | tf_op jit(solution)/shard_map/ppermute | solution.py:22
  336.9 5.8 %collective-permute-start.56 = (f32[4,2,1,128]{3,2,0,1:T(1,128)S(1)}, f32[4,2,1,128]{3,2,0,1:T(1,128)S(1)}, u32[]{:S(2)}, u32[]{:S(2)}) collective-permute-start(f32[4,2,1,128]{3,2,0,1:T(1,128)S(1)} %get-tuple-element.88), channel_id=1, source_target_pairs={{0,8},{8,16},{16,24},{24,32},{32,40},{40,48},{48,56},{56,64},{64,7... | collective-permute-start | bytes 12296 | tf_op jit(solution)/shard_map/ppermute | solution.py:21
  340.8 4.9 collective-permute-start.57
  345.9 7.4 %collective-permute-start.58 = (f32[4,2,66,1]{3,2,0,1:T(8,128)S(1)}, f32[4,2,66,1]{3,2,0,1:T(8,128)S(1)}, u32[]{:S(2)}, u32[]{:S(2)}) collective-permute-start(f32[4,2,66,1]{3,2,0,1:T(8,128)S(1)} %get-tuple-element.56), channel_id=1, source_target_pairs={{0,1},{1,2},{2,3},{3,4},{4,5},{5,6},{6,7},{8,9},{9,10},{10,11},{11... | collective-permute-start | bytes 6344 | tf_op jit(solution)/shard_map/ppermute | solution.py:21
  347.9 11.9 %collective-permute-start.59 = (f32[4,2,66,1]{3,2,0,1:T(8,128)S(1)}, f32[4,2,66,1]{3,2,0,1:T(8,128)S(1)}, u32[]{:S(2)}, u32[]{:S(2)}) collective-permute-start(f32[4,2,66,1]{3,2,0,1:T(8,128)S(1)} %get-tuple-element.57), channel_id=1, source_target_pairs={{1,0},{2,1},{3,2},{4,3},{5,4},{6,5},{7,6},{9,8},{10,9},{11,10},{12... | collective-permute-start | bytes 6344 | tf_op jit(solution)/shard_map/ppermute | solution.py:22
  360.8 5.4 %collective-permute-start.60 = (f32[4,2,1,128]{3,2,0,1:T(1,128)S(1)}, f32[4,2,1,128]{3,2,0,1:T(1,128)S(1)}, u32[]{:S(2)}, u32[]{:S(2)}) collective-permute-start(f32[4,2,1,128]{3,2,0,1:T(1,128)S(1)} %get-tuple-element.86), channel_id=1, source_target_pairs={{0,8},{8,16},{16,24},{24,32},{32,40},{40,48},{48,56},{56,64},{64,7... | collective-permute-start | bytes 12296 | tf_op jit(solution)/shard_map/ppermute | solution.py:21
  364.3 4.9 collective-permute-start.61
  369.5 7.4 %collective-permute-start.62 = (f32[4,2,66,1]{3,2,0,1:T(8,128)S(1)}, f32[4,2,66,1]{3,2,0,1:T(8,128)S(1)}, u32[]{:S(2)}, u32[]{:S(2)}) collective-permute-start(f32[4,2,66,1]{3,2,0,1:T(8,128)S(1)} %get-tuple-element.54), channel_id=1, source_target_pairs={{0,1},{1,2},{2,3},{3,4},{4,5},{5,6},{6,7},{8,9},{9,10},{10,11},{11... | collective-permute-start | bytes 6344 | tf_op jit(solution)/shard_map/ppermute | solution.py:21
  371.4 11.9 %collective-permute-start.63 = (f32[4,2,66,1]{3,2,0,1:T(8,128)S(1)}, f32[4,2,66,1]{3,2,0,1:T(8,128)S(1)}, u32[]{:S(2)}, u32[]{:S(2)}) collective-permute-start(f32[4,2,66,1]{3,2,0,1:T(8,128)S(1)} %get-tuple-element.55), channel_id=1, source_target_pairs={{1,0},{2,1},{3,2},{4,3},{5,4},{6,5},{7,6},{9,8},{10,9},{11,10},{12... | collective-permute-start | bytes 6344 | tf_op jit(solution)/shard_map/ppermute | solution.py:22
  384.4 4.8 collective-permute-start.64
  387.3 4.9 collective-permute-start.65
  392.4 7.4 %collective-permute-start.66 = (f32[4,2,66,1]{3,2,1,0:T(8,128)S(1)}, f32[4,2,66,1]{3,2,1,0:T(8,128)S(1)}, u32[]{:S(2)}, u32[]{:S(2)}) collective-permute-start(f32[4,2,66,1]{3,2,1,0:T(8,128)S(1)} %get-tuple-element.52), channel_id=1, source_target_pairs={{0,1},{1,2},{2,3},{3,4},{4,5},{5,6},{6,7},{8,9},{9,10},{10,11},{11... | collective-permute-start | bytes 6344 | tf_op jit(solution)/shard_map/ppermute | solution.py:21
  394.4 11.9 %collective-permute-start.67 = (f32[4,2,66,1]{3,2,1,0:T(8,128)S(1)}, f32[4,2,66,1]{3,2,1,0:T(8,128)S(1)}, u32[]{:S(2)}, u32[]{:S(2)}) collective-permute-start(f32[4,2,66,1]{3,2,1,0:T(8,128)S(1)} %get-tuple-element.53), channel_id=1, source_target_pairs={{1,0},{2,1},{3,2},{4,3},{5,4},{6,5},{7,6},{9,8},{10,9},{11,10},{12... | collective-permute-start | bytes 6344 | tf_op jit(solution)/shard_map/ppermute | solution.py:22
  (12 other events, 43.9 us)
where the time goes:
time: 497 us; the launch traced here: 494 us
  waiting for transfers between devices  229 us (46%)
  starting transfers between devices  152 us (31%)
  blocking collectives  81.4 us (16%)
  other arithmetic  21.1 us (4%)
  local copies, waits for them, and re-layouts  7.62 us (2%)
    ppermute x34, waiting for transfers between devices, extended(): after = lax.ppermute(first, axis, down)  161 us
    ppermute x34, starting transfers between devices, extended(): before = lax.ppermute(last, axis, up)  94 us
    psum x1, blocking collectives, body(): gram = lax.psum(placed, ('probe', 'gx', 'gy')) / total_cells  74.6 us
    ppermute x34, waiting for transfers between devices, extended(): before = lax.ppermute(last, axis, up)  67.2 us
    ppermute x34, starting transfers between devices, extended(): after = lax.ppermute(first, axis, down)  58.2 us
  transfers between devices with their start and end apart: 68, of which 50 were waited for; matrix products, arithmetic and copies ran while one was open for 0% of the time, Pallas kernels for 0%

commit v1 on v0

v1 whole, which is shorter than its diff:
```python
import functools

import jax
import jax.numpy as jnp
from jax import lax
from jax.experimental import pallas as pl
from jax.experimental.pallas import tpu as pltpu
from jax.sharding import PartitionSpec as P

SWEEPS = 9
OMEGA = 0.6
DRAG = 0.05
PRIOR = 0.05

HALF = 4
ROWS, COLS = 64, 128
HALO = 2 * (SWEEPS - 1)
BI, BJ = (ROWS + 2 * HALO) // 8, (COLS + 2 * HALO) // 32
EXT = ROWS + 2 * HALO
ETA_HALO = 24
MESH = pl.DeviceIdType.MESH
F32 = jnp.float32
AROUND = ((-1, 0), (1, 0), (0, -1), (0, 1), (-1, -1), (-1, 1), (1, -1), (1, 1))


def lanes():
    return lax.broadcasted_iota(jnp.int32, (8, 128), 1)


def sublanes():
    return lax.broadcasted_iota(jnp.int32, (8, 128), 0)


def turn(x, shift, axis):
    shift = shift % x.shape[axis]
    return pltpu.roll(x, shift, axis) if shift else x


def pick(x, index):
    return jnp.take_along_axis(x, index, axis=1, mode="promise_in_bounds")


def unrolled(count, body):
    def step(i, carry):
        body(i)
        return carry

    lax.fori_loop(0, count, step, 0, unroll=True)


def pack_strips(ext, eta, left, right, eta_left, eta_right):
    lane = lax.broadcasted_iota(jnp.int32, (ROWS, COLS), 1)
    for f in range(8):
        own = ext[f, HALO : HALO + ROWS, :]
        here = (lane >= 16 * f) & (lane < 16 * f + 16)
        first, last = turn(own, 16 * f, 1), turn(own, 16 * f + 16, 1)
        left[...] = first if f == 0 else jnp.where(here, first, left[...])
        right[...] = last if f == 0 else jnp.where(here, last, right[...])
    lane = lax.broadcasted_iota(jnp.int32, (16, COLS), 1)
    first = last = None
    for g in range(4):
        own = eta[ETA_HALO + 16 * g : ETA_HALO + 16 * g + 16, :]
        here = (lane >= 32 * g) & (lane < 32 * g + 32)
        a, b = turn(own, 32 * g, 1), turn(own, 32 * g + 32, 1)
        first = a if g == 0 else jnp.where(here, a, first)
        last = b if g == 0 else jnp.where(here, b, last)
    eta_left[...] = first
    eta_right[...] = last


def relayout(ext, west, east, eta, eta_west, eta_east, side, eta_side, spread, eta_spread):
    lane = lanes()
    block = lane & 31
    group = lane >> 5
    wide = lax.broadcasted_iota(jnp.int32, (EXT, COLS), 1)
    w, e = west[...], east[...]
    side[0] = jnp.where(wide < 64, w, turn(e, 64, 1))
    side[1] = jnp.where(wide < 64, turn(w, 64, 1), e)
    for k in range(14):
        own_row = 8 * k - ETA_HALO
        slot = 0 if own_row < 0 else (1 if own_row < ROWS else 2)
        row = own_row - ROWS * (slot - 1)
        g, r = row // 16, row % 16
        a = turn(eta_west[slot, r : r + 8, :], -32 * g, 1)
        b = turn(eta_east[slot, r : r + 8, :], 32 - 32 * g, 1)
        eta_side[8 * k : 8 * k + 8, :] = jnp.where(lane < 32, a, b)

    def places(j):
        col = BJ * block + j - HALO
        own = jnp.clip(col, 0, COLS - 1)
        outside = (col < 0) | (col >= COLS)
        return col, own, outside

    def fields(i):
        rows = pl.ds(i, 8, stride=BI)
        own = [ext[f, rows, :] for f in range(8)]
        low, high = side[0, rows, :], side[1, rows, :]
        for j in range(BJ):
            col, at, outside = places(j)
            near_side = jnp.where(outside, jnp.where(col < 0, col + HALO, col - COLS + 64), 0)
            value = pick(own[HALF - 1], at)
            for p in range(HALF - 2, -1, -1):
                value = jnp.where(group == p, pick(own[p], at), value)
            spread[0, i, j] = jnp.where(outside, pick(low, near_side + 16 * group), value)
            for f in range(4):
                spread[1 + f, i, j] = jnp.where(outside, pick(high, near_side + 16 * f), pick(own[4 + f], at))

    unrolled(BI, fields)

    def viscosity(i):
        rows = pl.ds(i + ETA_HALO - HALO - 1, 8, stride=BI)
        own, beside = eta[rows, :], eta_side[rows, :]
        for j in range(-1, BJ + 1):
            col, at, outside = places(j)
            near_side = jnp.where(outside, jnp.where(col < 0, col + 32, col - COLS + 32), 0)
            eta_spread[i, j + 1] = jnp.where(outside, pick(beside, near_side), pick(own, at))

    unrolled(BI + 2, viscosity)


def store_state(state, c, i, values):
    values = [turn(values[BJ - 1], 1, 1)] + values + [turn(values[0], -1, 1)]
    for j, value in enumerate(values):
        state[c, i + 1, j] = value

    def before(i):
        for j, value in enumerate(values):
            state[c, 0, j] = turn(value, 1, 0)

    def after(i):
        for j, value in enumerate(values):
            state[c, BI + 1, j] = turn(value, -1, 0)

    return before, after


def wrap_rows(state):
    for c in range(2):
        for j in range(BJ + 2):
            state[c, 0, j] = turn(state[c, BI, j], 1, 0)
            state[c, BI + 1, j] = turn(state[c, 1, j], -1, 0)


def coefficients(spread, eta_spread, coef, weight, source, state, gx, gy, nx, ny):
    lane, sub = lanes(), sublanes()

    def row(i):
        r = gx * ROWS - HALO + BI * sub + i
        row_in = (r >= 0) & (r < nx)
        first, second = [], []
        for j in range(BJ):
            c = gy * COLS - HALO + BJ * (lane & 31) + j
            inside = row_in & (c >= 0) & (c < ny)
            m = eta_spread[i + 1, j + 1]
            e, w = eta_spread[i + 2, j + 1], eta_spread[i, j + 1]
            n, s = eta_spread[i + 1, j + 2], eta_spread[i + 1, j]
            react = spread[3, i, j] + DRAG
            me, mw, mn, ms = m + e, m + w, m + n, m + s
            along, across = me + mw, mn + ms
            w1 = jnp.where(inside, OMEGA / (2.0 * along + 0.5 * across + react), 0.0)
            w2 = jnp.where(inside, OMEGA / (0.5 * along + 2.0 * across + react), 0.0)
            a1, b1, q1 = 2.0 * w1, 0.5 * w1, 0.25 * w1
            a2, b2, q2 = 2.0 * w2, 0.5 * w2, 0.25 * w2
            coef[0, i, j] = a1 * me
            coef[1, i, j] = a1 * mw
            coef[2, i, j] = b1 * mn
            coef[3, i, j] = b1 * ms
            be, bw, qn, qs = b1 * e, b1 * w, q1 * n, q1 * s
            coef[4, i, j] = be + qn
            coef[5, i, j] = be + qs
            coef[6, i, j] = bw + qn
            coef[7, i, j] = bw + qs
            coef[8, i, j] = b2 * me
            coef[9, i, j] = b2 * mw
            coef[10, i, j] = a2 * mn
            coef[11, i, j] = a2 * ms
            bn, bs, qe, qw = b2 * n, b2 * s, q2 * e, q2 * w
            coef[12, i, j] = bn + qe
            coef[13, i, j] = bs + qe
            coef[14, i, j] = bn + qw
            coef[15, i, j] = bs + qw
            noise = spread[4, i, j]
            weight[0, i, j] = w1 * noise
            weight[1, i, j] = w2 * noise
            probe = spread[0, i, j]
            f1, f2 = w1 * (spread[1, i, j] * probe), w2 * (spread[2, i, j] * probe)
            source[0, i, j] = f1
            source[1, i, j] = f2
            first.append(f1)
            second.append(f2)
        store_state(state, 0, i, first)
        store_state(state, 1, i, second)

    unrolled(BI, row)
    wrap_rows(state)


def sweep(old, new, coef, source):
    def row(i):
        first, second = [], []
        for j in range(BJ):

            def at(c, di, dj):
                return old[c, i + 1 + di, j + 1 + dj]

            k = [coef[n, i, j] for n in range(16)]
            first.append(
                (0.4 * at(0, 0, 0) + source[0, i, j])
                + (k[0] * at(0, 1, 0) + k[1] * at(0, -1, 0))
                + (k[2] * at(0, 0, 1) + k[3] * at(0, 0, -1))
                + (k[4] * at(1, 1, 1) - k[5] * at(1, 1, -1))
                + (k[7] * at(1, -1, -1) - k[6] * at(1, -1, 1))
            )
            second.append(
                (0.4 * at(1, 0, 0) + source[1, i, j])
                + (k[8] * at(1, 1, 0) + k[9] * at(1, -1, 0))
                + (k[10] * at(1, 0, 1) + k[11] * at(1, 0, -1))
                + (k[12] * at(0, 1, 1) - k[13] * at(0, 1, -1))
                + (k[15] * at(0, -1, -1) - k[14] * at(0, -1, 1))
            )
        store_state(new, 0, i, first)
        store_state(new, 1, i, second)

    unrolled(BI, row)
    wrap_rows(new)


def relax(state_a, state_b, coef, source):
    def two(k, carry):
        sweep(state_a, state_b, coef, source)
        sweep(state_b, state_a, coef, source)
        return carry

    lax.fori_loop(0, (SWEEPS - 1) // 2, two, 0)


def next_source(state, weight, source):
    def row(i):
        for c in range(2):
            values = [weight[c, i, j] * state[c, i + 1, j + 1] for j in range(BJ)]
            for j in range(BJ):
                source[c, i, j] = values[j]
            store_state(state, c, i, values)

    unrolled(BI, row)
    wrap_rows(state)


def gather_images(state, spread, natural):
    lane = lanes()
    place = lane + HALO
    block = (place * 205) >> 10
    rest = place - BJ * block

    def row(i):
        values = [
            spread[1, i, j] * state[0, i + 1, j + 1]
            + spread[2, i, j] * state[1, i + 1, j + 1]
            + PRIOR * spread[0, i, j]
            for j in range(BJ)
        ]
        for p in range(HALF):
            out = pick(values[0], block + 32 * p)
            for j in range(1, BJ):
                out = jnp.where(rest == j, pick(values[j], block + 32 * p), out)
            natural[p, pl.ds(i, 8, stride=BI), :] = out

    unrolled(BI, row)


def products(left, left_row, right, right_row):
    def add(k, totals):
        a = [left[p, pl.ds(left_row + 8 * k, 8), :] for p in range(HALF)]
        b = [right[p, pl.ds(right_row + 8 * k, 8), :] for p in range(HALF)]
        return tuple(t + a[n // 4] * b[n % 4] for n, t in enumerate(totals))

    zero = jnp.zeros((8, 128), F32)
    totals = lax.fori_loop(0, ROWS // 8, add, (zero,) * 16, unroll=True)
    sums = jnp.concatenate([jnp.sum(t, axis=0, keepdims=True) for t in totals], axis=0)
    sums = jnp.sum(sums, axis=1, keepdims=True)
    lane = lax.broadcasted_iota(jnp.int32, (16, 128), 1)
    row = lax.broadcasted_iota(jnp.int32, (16, 128), 0)
    return jnp.sum(jnp.where(lane == row, sums, 0.0), axis=0, keepdims=True)


def main_kernel(
    nx_devices, ny_devices,
    probes, velocity, eta_in, friction, noise, ice,
    images, other_images, gram,
    ext, west, east, left, right, eta, eta_west, eta_east, eta_left, eta_right,
    vel, fric, mask, side, eta_side, spread, eta_spread, coef, weight, source, state_a, state_b,
    natural, other_probes, message, inbox_a, inbox_b,
    in_sem, halo_send, halo_recv, eta_send, eta_recv, pair_send, pair_recv,
    a_send, a_recv, b_send, b_recv,
):
    half, gx, gy = lax.axis_index("probe"), lax.axis_index("gx"), lax.axis_index("gy")
    group_a, group_b = nx_devices, 2 * ny_devices
    me_b = gy * 2 + half
    own_rows = slice(HALO, HALO + ROWS)

    loads = [
        pltpu.make_async_copy(velocity, vel, in_sem.at[0]),
        pltpu.make_async_copy(friction, fric, in_sem.at[1]),
        pltpu.make_async_copy(ice, mask, in_sem.at[2]),
        pltpu.make_async_copy(probes, ext.at[0:HALF, own_rows, :], in_sem.at[3]),
        pltpu.make_async_copy(noise, ext.at[7, own_rows, :], in_sem.at[4]),
        pltpu.make_async_copy(eta_in, eta.at[ETA_HALO : ETA_HALO + ROWS, :], in_sem.at[5]),
    ]
    for load in loads:
        load.start()

    def blank(ref):
        ref[...] = jnp.zeros(ref.shape, F32)

    @pl.when(gx == 0)
    def _():
        blank(ext.at[:, 0:HALO, :])
        blank(eta.at[0:ETA_HALO, :])
        for ref in (west, east):
            blank(ref.at[0:HALO, :])
        for ref in (eta_west, eta_east):
            blank(ref.at[0])

    @pl.when(gx == nx_devices - 1)
    def _():
        blank(ext.at[:, HALO + ROWS : EXT, :])
        blank(eta.at[ETA_HALO + ROWS : 2 * ETA_HALO + ROWS, :])
        for ref in (west, east):
            blank(ref.at[HALO + ROWS : EXT, :])
        for ref in (eta_west, eta_east):
            blank(ref.at[2])

    @pl.when(gy == 0)
    def _():
        blank(west)
        blank(eta_west)

    @pl.when(gy == ny_devices - 1)
    def _():
        blank(east)
        blank(eta_east)

    def exists(dx, dy):
        x, y = gx + dx, gy + dy
        return (x >= 0) & (x < nx_devices) & (y >= 0) & (y < ny_devices)

    def at_b(t):
        return {"probe": lax.rem(t, 2), "gy": lax.div(t, 2)}

    barrier = pltpu.get_barrier_semaphore()
    for dx, dy in AROUND:

        @pl.when(exists(dx, dy))
        def _():
            pl.semaphore_signal(barrier, inc=1, device_id={"gx": gx + dx, "gy": gy + dy}, device_id_type=MESH)

    def greet_a(k, carry):
        pl.semaphore_signal(barrier, inc=1, device_id={"gx": lax.rem(gx + k, group_a)}, device_id_type=MESH)
        return carry

    def greet_b(k, carry):
        pl.semaphore_signal(barrier, inc=1, device_id=at_b(lax.rem(me_b + k, group_b)), device_id_type=MESH)
        return carry

    lax.fori_loop(1, group_a, greet_a, 0)
    lax.fori_loop(1, group_b, greet_b, 0)

    for load in loads:
        load.wait()
    coupling = fric[...] * mask[...].astype(F32)
    ext[4, own_rows, :] = -coupling * vel[0]
    ext[5, own_rows, :] = -coupling * vel[1]
    ext[6, own_rows, :] = coupling
    pack_strips(ext, eta, left, right, eta_left, eta_right)

    tall = jnp.where((gx > 0) & (gx < nx_devices - 1), 3, jnp.where(nx_devices > 1, 2, 1))
    long = jnp.where((gy > 0) & (gy < ny_devices - 1), 3, jnp.where(ny_devices > 1, 2, 1))
    pl.semaphore_wait(barrier, tall * long - 1 + (group_a - 1) + (group_b - 1))

    def halo_copies(n):
        dx, dy = AROUND[n]
        to = {"gx": gx + dx, "gy": gy + dy}
        if dy == 0:
            src_row, dst_row = (ROWS, 0) if dx > 0 else (HALO, HALO + ROWS)
            main = (ext.at[:, src_row : src_row + HALO, :], ext.at[:, dst_row : dst_row + HALO, :])
            src_row, dst_row = (ROWS, 0) if dx > 0 else (ETA_HALO, ETA_HALO + ROWS)
            more = (eta.at[src_row : src_row + ETA_HALO, :], eta.at[dst_row : dst_row + ETA_HALO, :])
        else:
            strip, landing = (right, west) if dy > 0 else (left, east)
            src_row, dst_row, count = {0: (0, HALO, ROWS), 1: (ROWS - HALO, 0, HALO), -1: (0, HALO + ROWS, HALO)}[dx]
            main = (strip.at[src_row : src_row + count, :], landing.at[dst_row : dst_row + count, :])
            strip, landing = (eta_right, eta_west) if dy > 0 else (eta_left, eta_east)
            more = (strip, landing.at[1 - dx])
        return [
            pltpu.make_async_remote_copy(
                src_ref=src, dst_ref=dst, send_sem=sends.at[n], recv_sem=recvs.at[n], device_id=to, device_id_type=MESH
            )
            for (src, dst), sends, recvs in ((main, halo_send, halo_recv), (more, eta_send, eta_recv))
        ]

    for n, (dx, dy) in enumerate(AROUND):

        @pl.when(exists(dx, dy))
        def _():
            for copy in halo_copies(n):
                copy.start()

    probe_copy = pltpu.make_async_remote_copy(
        src_ref=ext.at[0:HALF, own_rows, :], dst_ref=other_probes,
        send_sem=pair_send.at[0], recv_sem=pair_recv.at[0], device_id={"probe": 1 - half}, device_id_type=MESH,
    )
    image_copy = pltpu.make_async_remote_copy(
        src_ref=natural.at[:, own_rows, :], dst_ref=other_images,
        send_sem=pair_send.at[1], recv_sem=pair_recv.at[1], device_id={"probe": 1 - half}, device_id_type=MESH,
    )

    @pl.when(half == 1)
    def _():
        probe_copy.start()

    for n, (dx, dy) in enumerate(AROUND):

        @pl.when(exists(-dx, -dy))
        def _():
            for copy in halo_copies(n):
                copy.wait_recv()

    relayout(ext, west, east, eta, eta_west, eta_east, side, eta_side, spread, eta_spread)
    coefficients(
        spread, eta_spread, coef, weight, source, state_a, gx, gy, nx_devices * ROWS, ny_devices * COLS
    )
    relax(state_a, state_b, coef, source)
    next_source(state_a, weight, source)
    relax(state_a, state_b, coef, source)
    gather_images(state_a, spread, natural)

    @pl.when(half == 0)
    def _():
        image_copy.start()

    own = products(ext, HALO, natural, HALO)

    @pl.when(half == 0)
    def _():
        probe_copy.wait_recv()
        cross = products(other_probes, 0, natural, HALO)
        message[0] = jnp.broadcast_to(own + turn(cross, 16, 1), (8, 128))

    @pl.when(half == 1)
    def _():
        message[0] = jnp.broadcast_to(turn(own, 32, 1), (8, 128))

    def reduce(phase, inbox, me, count, sends, recvs, place):
        def copy_to(k):
            return pltpu.make_async_remote_copy(
                src_ref=message.at[phase], dst_ref=inbox.at[me], send_sem=sends.at[k], recv_sem=recvs.at[me],
                device_id=place(lax.rem(me + k, count)), device_id_type=MESH,
            )

        def copy_from(k):
            return pltpu.make_async_remote_copy(
                src_ref=message.at[phase], dst_ref=inbox.at[k], send_sem=sends.at[0], recv_sem=recvs.at[k],
                device_id=place(k), device_id_type=MESH,
            )

        def send(k, carry):
            copy_to(k).start()
            return carry

        def receive(k, carry):
            copy_from(lax.rem(me + k, count)).wait_recv()
            return carry

        def sent(k, carry):
            copy_to(k).wait_send()
            return carry

        lax.fori_loop(1, count, send, 0)
        inbox[me] = message[phase]
        lax.fori_loop(1, count, receive, 0)
        total = inbox[0]
        for k in range(1, count):
            total = total + inbox[k]
        return total, lambda: lax.fori_loop(1, count, sent, 0)

    total, done_a = reduce(0, inbox_a, gx, group_a, a_send, a_recv, lambda t: {"gx": t})
    message[1] = total
    total, done_b = reduce(1, inbox_b, me_b, group_b, b_send, b_recv, at_b)
    gram[...] = total * (1.0 / (nx_devices * ROWS * ny_devices * COLS))
    images[...] = natural[:, own_rows, :]

    for n, (dx, dy) in enumerate(AROUND):

        @pl.when(exists(dx, dy))
        def _():
            for copy in halo_copies(n):
                copy.wait_send()

    done_a()
    done_b()

    @pl.when(half == 0)
    def _():
        image_copy.wait_send()

    @pl.when(half == 1)
    def _():
        probe_copy.wait_send()
        image_copy.wait_recv()


def last_kernel(sums, images, other_images, images_out, factor, gram):
    half = lax.axis_index("probe")

    def entry(i, j):
        i, j = max(i, j), min(i, j)
        if i < HALF:
            return sums[0, 4 * i + j]
        if j < HALF:
            return sums[0, 16 + 4 * (i - HALF) + j]
        return sums[0, 32 + 4 * (i - HALF) + j - HALF]

    count = 2 * HALF
    g = {(i, j): jnp.full((8, 128), entry(i, j), F32) for i in range(count) for j in range(i + 1)}
    for i in range(count):
        for j in range(i):
            if (i < HALF) == (j < HALF):
                k = 4 * (j % HALF) + i % HALF + (0 if i < HALF else 32)
                g[i, j] = 0.5 * (g[i, j] + jnp.full((8, 128), sums[0, k], F32))
    lane, sub = lanes(), sublanes()
    out = jnp.zeros((8, 128), F32)
    for i in range(count):
        row = jnp.zeros((8, 128), F32)
        for j in range(count):
            a, b = i % HALF, j % HALF
            if (i < HALF) == (j < HALF):
                value = sums[0, 4 * a + b + (0 if i < HALF else 32)]
            else:
                value = entry(i, j)
            row = jnp.where(lane == j, value, row)
        out = jnp.where(sub == i, row, out)
    gram[...] = out[:, :count]

    low, inverse = {}, {}
    for j in range(count):
        for i in range(j, count):
            value = g[i, j]
            for k in range(j):
                value = value - low[i, k] * low[j, k]
            if i == j:
                root = jnp.sqrt(value)
                inverse[j] = 1.0 / root
            else:
                low[i, j] = value * inverse[j]

    def solve(sources, out_rows):
        def part(k):
            rows = pl.ds(8 * k, 8)
            done = []
            for i, (ref, p) in enumerate(sources):
                value = ref[p, rows, :]
                for j in range(i):
                    value = value - low[i, j] * done[j]
                value = value * inverse[i]
                done.append(value)
                if i >= len(sources) - HALF:
                    factor[i - len(sources) + HALF, rows, :] = value

        unrolled(ROWS // 8, part)

    images_out[...] = images[...]

    @pl.when(half == 0)
    def _():
        solve([(images, p) for p in range(HALF)], 0)

    @pl.when(half == 1)
    def _():
        solve([(other_images, p) for p in range(HALF)] + [(images, p) for p in range(HALF)], HALF)


def body(probes, velocity, eta, friction, noise, ice):
    nx_devices, ny_devices = lax.axis_size("gx"), lax.axis_size("gy")
    vmem = lambda *shape: pltpu.VMEM(shape, F32)
    dma = lambda count: pltpu.SemaphoreType.DMA((count,))
    grid = (BI, BJ, 8, 128)
    padded = (BI + 2, BJ + 2, 8, 128)
    whole = pl.BlockSpec(memory_space=pltpu.VMEM)
    tile = jax.ShapeDtypeStruct((HALF, ROWS, COLS), F32)
    group_a, group_b = nx_devices, 2 * ny_devices
    images, other_images, sums = pl.pallas_call(
        functools.partial(main_kernel, nx_devices, ny_devices),
        out_shape=(tile, tile, jax.ShapeDtypeStruct((8, 128), F32)),
        in_specs=[pl.BlockSpec(memory_space=pl.ANY)] * 6,
        out_specs=(whole, whole, whole),
        scratch_shapes=[
            vmem(8, EXT, 128), vmem(EXT, 128), vmem(EXT, 128), vmem(ROWS, 128), vmem(ROWS, 128),
            vmem(ROWS + 2 * ETA_HALO, 128), vmem(3, 16, 128), vmem(3, 16, 128), vmem(16, 128), vmem(16, 128),
            vmem(2, ROWS, COLS), vmem(ROWS, COLS), pltpu.VMEM((ROWS, COLS), jnp.int32),
            vmem(2, EXT, 128), vmem(ROWS + 2 * ETA_HALO, 128),
            vmem(5, *grid), vmem(*padded), vmem(16, *grid), vmem(2, *grid), vmem(2, *grid),
            vmem(2, *padded), vmem(2, *padded),
            vmem(HALF, EXT, 128), vmem(HALF, ROWS, COLS), vmem(2, 8, 128), vmem(group_a, 8, 128), vmem(group_b, 8, 128),
            dma(6), dma(8), dma(8), dma(8), dma(8), dma(2), dma(2),
            dma(group_a), dma(group_a), dma(group_b), dma(group_b),
        ],
        compiler_params=pltpu.CompilerParams(
            collective_id=0, has_side_effects=True, vmem_limit_bytes=32 * 1024 * 1024
        ),
    )(probes, velocity, eta, friction, noise, ice)
    return pl.pallas_call(
        last_kernel,
        out_shape=(tile, tile, jax.ShapeDtypeStruct((2 * HALF, 2 * HALF), F32)),
        in_specs=[pl.BlockSpec(memory_space=pltpu.SMEM), whole, whole],
        out_specs=(whole, whole, whole),
    )(sums, images, other_images)


def solution(mesh):
    in_specs = (
        P("probe", "gx", "gy"),
        P(None, "gx", "gy"),
        P("gx", "gy"),
        P("gx", "gy"),
        P("gx", "gy"),
        P("gx", "gy"),
    )
    out_specs = (P("probe", "gx", "gy"), P("probe", "gx", "gy"), P())
    return jax.shard_map(body, mesh=mesh, in_specs=in_specs, out_specs=out_specs, check_vma=False)
```

time: 497 us -> 46.3 us (0.09)
  waiting for transfers between devices: 229 us -> 0 us
  starting transfers between devices: 152 us -> 0 us
  blocking collectives: 81.4 us -> 0 us
  Pallas kernels: 0 us -> 38.6 us
  other arithmetic: 21.1 us -> 0 us
    ppermute x68 -> x0, waiting for transfers between devices: 229 us -> none  [the longest x34 161 us: extended(): after = lax.ppermute(first, axis, down)]
    ppermute x68 -> x0, starting transfers between devices: 152 us -> none  [the longest x34 94 us: extended(): before = lax.ppermute(last, axis, up)]
    psum x1 -> x0, blocking collectives: 74.6 us -> none  [body(): gram = lax.psum(placed, ('probe', 'gx', 'gy')) / total_cells]
    pallas_call x0 -> x2, Pallas kernels: none -> 38.6 us  [the longest x1 36.7 us: body(): pl.pallas_call(functools.partial(main_kernel, nx_devices, ny_devices), ou...]
    another operation x39 -> x0, other arithmetic: 12.2 us -> none  [the longest x32 9.38 us: stencil(): return jnp.stack([first, second], axis=-3)]
    all_gather x1 -> x0, blocking collectives: 6.81 us -> none  [body(): gathered = lax.all_gather(images, 'probe', axis=0, tiled=True)]
    concatenate x33 -> x0, other arithmetic: 6.56 us -> none  [extended(): x = jnp.concatenate([before, x, after], axis=dim)]
  transfers between devices with their start and end apart: 68 -> 0, of which waited for: 50 -> 0; matrix products, arithmetic and copies ran while one was open for 0% -> 0% of each run, Pallas kernels for 0% -> 0%
where the time goes in v1:
time: 46.3 us; the launch traced here: 45.9 us
  Pallas kernels  38.6 us (83%)
  local copies, waits for them, and re-layouts  6.65 us (14%)
  between operations  0.66 us (1%)
    pallas_call x1, Pallas kernels, body(): pl.pallas_call(functools.partial(main_kernel, nx_devices, ny_devices), ou...  36.7 us
    unnamed x18, local copies, waits for them, and re-layouts  6.65 us
    pallas_call x1, Pallas kernels, body(): pl.pallas_call(last_kernel, out_shape=(tile, tile, jax.ShapeDtypeStruct((...  1.85 us

profile of v1, /device:TPU:1, one launch (start us, length us, event | category | flops | bytes accessed | tf_op | source)
XLA Modules:
  0.0 45.9 jit_solution(7989189338980863144)
XLA Ops:
  0.6 0.0 copy-start
  0.6 0.9 %copy-done = f32[4,64,128]{2,1,0:T(8,128)S(1)} copy-done((f32[4,64,128]{2,1,0:T(8,128)S(1)}, f32[4,64,128]{2,1,0:T(8,128)}, u32[]{:S(2)}) %copy-start) | copy-done | bytes 131096
  1.5 0.0 copy-start.3
  1.5 0.8 %copy-done.3 = f32[2,64,128]{2,1,0:T(8,128)S(1)} copy-done((f32[2,64,128]{2,1,0:T(8,128)S(1)}, f32[2,64,128]{2,1,0:T(8,128)}, u32[]{:S(2)}) %copy-start.3) | copy-done | bytes 65560
  2.4 0.0 copy-start.4
  2.4 0.8 %copy-done.4 = f32[64,128]{1,0:T(8,128)S(1)} copy-done((f32[64,128]{1,0:T(8,128)S(1)}, f32[64,128]{1,0:T(8,128)}, u32[]{:S(2)}) %copy-start.4) | copy-done | bytes 32792
  3.1 0.0 copy-start.5
  3.1 0.8 %copy-done.5 = f32[64,128]{1,0:T(8,128)S(1)} copy-done((f32[64,128]{1,0:T(8,128)S(1)}, f32[64,128]{1,0:T(8,128)}, u32[]{:S(2)}) %copy-start.5) | copy-done | bytes 32792
  3.9 0.0 copy-start.6
  3.9 0.8 %copy-done.6 = f32[64,128]{1,0:T(8,128)S(1)} copy-done((f32[64,128]{1,0:T(8,128)S(1)}, f32[64,128]{1,0:T(8,128)}, u32[]{:S(2)}) %copy-start.6) | copy-done | bytes 32792
  4.7 0.0 copy-start.7
  4.7 0.8 %copy-done.7 = s32[64,128]{1,0:T(8,128)S(1)} copy-done((s32[64,128]{1,0:T(8,128)S(1)}, s32[64,128]{1,0:T(8,128)}, u32[]{:S(2)}) %copy-start.7) | copy-done | bytes 32792
  5.4 36.7 %shard_map.85 = (f32[4,64,128]{2,1,0:T(8,128)S(1)}, f32[4,64,128]{2,1,0:T(8,128)S(1)}, f32[8,128]{1,0:T(8,128)S(1)}) custom-call(f32[4,64,128]{2,1,0:T(8,128)S(1)} %copy-done, f32[2,64,128]{2,1,0:T(8,128)S(1)} %copy-done.3, f32[64,128]{1,0:T(8,128)S(1)} %copy-done.4, f32[64,128]{1,0:T(8,128)S(1)} %copy-done.5, f32[64,128]{1,0:T(8,128)S(1)} %copy-done.6, ...), custom_call_target="tpu_custom_call" | custom-call | tf_op jit(solution)/shard_map/pallas_call | solution.py:591
  42.1 0.0 copy-start.1
  42.2 0.6 %copy-done.1 = f32[4,64,128]{2,1,0:T(8,128)} copy-done((f32[4,64,128]{2,1,0:T(8,128)}, f32[4,64,128]{2,1,0:T(8,128)S(1)}, u32[]{:S(2)}) %copy-start.1) | copy-done | bytes 131096
  42.8 0.0 copy-start.2
  42.8 0.7 %copy-done.2 = f32[4,64,128]{2,1,0:T(8,128)} copy-done((f32[4,64,128]{2,1,0:T(8,128)}, f32[4,64,128]{2,1,0:T(8,128)S(1)}, u32[]{:S(2)}) %copy-start.2) | copy-done | bytes 131096
  43.4 0.0 copy-start.8
  43.4 0.6 %copy-done.8 = f32[8,128]{1,0:T(8,128)} copy-done((f32[8,128]{1,0:T(8,128)}, f32[8,128]{1,0:T(8,128)S(1)}, u32[]{:S(2)}) %copy-start.8) | copy-done | bytes 4120
  44.0 1.8 %shard_map.86 = (f32[4,64,128]{2,1,0:T(8,128)}, f32[4,64,128]{2,1,0:T(8,128)}, f32[8,8]{1,0:T(8,128)}) custom-call(f32[8,128]{1,0:T(8,128)} %copy-done.8, f32[4,64,128]{2,1,0:T(8,128)} %copy-done.1, f32[4,64,128]{2,1,0:T(8,128)} %copy-done.2), custom_call_target="tpu_custom_call" | custom-call | tf_op jit(solution)/shard_map/pallas_call | solution.py:611
Async XLA Ops:
  0.6 0.9 %copy-start = (f32[4,64,128]{2,1,0:T(8,128)S(1)}, f32[4,64,128]{2,1,0:T(8,128)}, u32[]{:S(2)}) copy-start(f32[4,64,128]{2,1,0:T(8,128)} %probes.1) | copy-start | bytes 393220
  1.5 0.8 %copy-start.3 = (f32[2,64,128]{2,1,0:T(8,128)S(1)}, f32[2,64,128]{2,1,0:T(8,128)}, u32[]{:S(2)}) copy-start(f32[2,64,128]{2,1,0:T(8,128)} %velocity.1) | copy-start | bytes 196612
  2.4 0.8 %copy-start.4 = (f32[64,128]{1,0:T(8,128)S(1)}, f32[64,128]{1,0:T(8,128)}, u32[]{:S(2)}) copy-start(f32[64,128]{1,0:T(8,128)} %eta_in.1) | copy-start | bytes 98308
  3.1 0.8 %copy-start.5 = (f32[64,128]{1,0:T(8,128)S(1)}, f32[64,128]{1,0:T(8,128)}, u32[]{:S(2)}) copy-start(f32[64,128]{1,0:T(8,128)} %friction.1) | copy-start | bytes 98308
  3.9 0.8 %copy-start.6 = (f32[64,128]{1,0:T(8,128)S(1)}, f32[64,128]{1,0:T(8,128)}, u32[]{:S(2)}) copy-start(f32[64,128]{1,0:T(8,128)} %noise.1) | copy-start | bytes 98308
  4.7 0.8 %copy-start.7 = (s32[64,128]{1,0:T(8,128)S(1)}, s32[64,128]{1,0:T(8,128)}, u32[]{:S(2)}) copy-start(s32[64,128]{1,0:T(8,128)} %ice.1) | copy-start | bytes 98308
  42.1 0.6 %copy-start.1 = (f32[4,64,128]{2,1,0:T(8,128)}, f32[4,64,128]{2,1,0:T(8,128)S(1)}, u32[]{:S(2)}) copy-start(f32[4,64,128]{2,1,0:T(8,128)S(1)} %get-tuple-element.7.images) | copy-start | bytes 393220
  42.8 0.7 %copy-start.2 = (f32[4,64,128]{2,1,0:T(8,128)}, f32[4,64,128]{2,1,0:T(8,128)S(1)}, u32[]{:S(2)}) copy-start(f32[4,64,128]{2,1,0:T(8,128)S(1)} %get-tuple-element.8.other_images) | copy-start | bytes 393220
  43.4 0.6 %copy-start.8 = (f32[8,128]{1,0:T(8,128)}, f32[8,128]{1,0:T(8,128)S(1)}, u32[]{:S(2)}) copy-start(f32[8,128]{1,0:T(8,128)S(1)} %get-tuple-element.6.sums) | copy-start | bytes 12292

commit v2 on v1

--- a/solution.py
+++ b/solution.py
@@ -2,6 +2,7 @@
 
 import jax
 import jax.numpy as jnp
+import numpy as np
 from jax import lax
 from jax.experimental import pallas as pl
 from jax.experimental.pallas import tpu as pltpu
@@ -20,6 +21,10 @@
 ETA_HALO = 24
 MESH = pl.DeviceIdType.MESH
 F32 = jnp.float32
+SERIES = np.polynomial.Polynomial([0.0])
+for power in range(SWEEPS):
+    SERIES = SERIES + np.polynomial.Polynomial([1.0 - OMEGA, OMEGA]) ** power
+SERIES = [float(a) for a in SERIES.coef]
 AROUND = ((-1, 0), (1, 0), (0, -1), (0, 1), (-1, -1), (-1, 1), (1, -1), (1, 1))
 
 
@@ -40,12 +45,18 @@
     return jnp.take_along_axis(x, index, axis=1, mode="promise_in_bounds")
 
 
-def unrolled(count, body):
+def unrolled(count, body, start=0):
     def step(i, carry):
         body(i)
         return carry
 
-    lax.fori_loop(0, count, step, 0, unroll=True)
+    lax.fori_loop(start, count, step, 0, unroll=True)
+
+
+def ends_first(body):
+    body(0)
+    body(BI - 1)
+    unrolled(BI - 1, body, 1)
 
 
 def pack_strips(ext, eta, left, right, eta_left, eta_right):
@@ -68,9 +79,38 @@
     eta_right[...] = last
 
 
-def relayout(ext, west, east, eta, eta_west, eta_east, side, eta_side, spread, eta_spread):
+def places(j):
+    col = BJ * (lanes() & 31) + j - HALO
+    return col, jnp.clip(col, 0, COLS - 1), (col < 0) | (col >= COLS)
+
+
+def relayout_own(ext, eta, spread, eta_spread):
+    group = lanes() >> 5
+
+    def fields(i):
+        rows = pl.ds(i, 8, stride=BI)
+        own = [ext[f, rows, :] for f in range(8)]
+        for j in range(BJ):
+            _, at, _ = places(j)
+            value = pick(own[HALF - 1], at)
+            for p in range(HALF - 2, -1, -1):
+                value = jnp.where(group == p, pick(own[p], at), value)
+            spread[0, i, j] = value
+            for f in range(4):
+                spread[1 + f, i, j] = pick(own[4 + f], at)
+
+    unrolled(BI, fields)
+
+    def viscosity(i):
+        own = eta[pl.ds(i + ETA_HALO - HALO - 1, 8, stride=BI), :]
+        for j in range(-1, BJ + 1):
+            eta_spread[i, j + 1] = pick(own, places(j)[1])
+
+    unrolled(BI + 2, viscosity)
+
+
+def relayout_sides(west, east, eta_west, eta_east, side, eta_side, spread, eta_spread):
     lane = lanes()
-    block = lane & 31
     group = lane >> 5
     wide = lax.broadcasted_iota(jnp.int32, (EXT, COLS), 1)
     w, e = west[...], east[...]
@@ -85,60 +125,38 @@
         b = turn(eta_east[slot, r : r + 8, :], 32 - 32 * g, 1)
         eta_side[8 * k : 8 * k + 8, :] = jnp.where(lane < 32, a, b)
 
-    def places(j):
-        col = BJ * block + j - HALO
-        own = jnp.clip(col, 0, COLS - 1)
-        outside = (col < 0) | (col >= COLS)
-        return col, own, outside
+    def viscosity(i):
+        beside = eta_side[pl.ds(i + ETA_HALO - HALO - 1, 8, stride=BI), :]
+        for j in range(-1, BJ + 1):
+            col, _, outside = places(j)
+            at = jnp.where(outside, jnp.where(col < 0, col + 32, col - COLS + 32), 0)
+            eta_spread[i, j + 1] = jnp.where(outside, pick(beside, at), eta_spread[i, j + 1])
+
+    unrolled(BI + 2, viscosity)
 
     def fields(i):
         rows = pl.ds(i, 8, stride=BI)
-        own = [ext[f, rows, :] for f in range(8)]
         low, high = side[0, rows, :], side[1, rows, :]
         for j in range(BJ):
-            col, at, outside = places(j)
-            near_side = jnp.where(outside, jnp.where(col < 0, col + HALO, col - COLS + 64), 0)
-            value = pick(own[HALF - 1], at)
-            for p in range(HALF - 2, -1, -1):
-                value = jnp.where(group == p, pick(own[p], at), value)
-            spread[0, i, j] = jnp.where(outside, pick(low, near_side + 16 * group), value)
+            col, _, outside = places(j)
+            at = jnp.where(outside, jnp.where(col < 0, col + HALO, col - COLS + 64), 0)
+            spread[0, i, j] = jnp.where(outside, pick(low, at + 16 * group), spread[0, i, j])
             for f in range(4):
-                spread[1 + f, i, j] = jnp.where(outside, pick(high, near_side + 16 * f), pick(own[4 + f], at))
+                spread[1 + f, i, j] = jnp.where(outside, pick(high, at + 16 * f), spread[1 + f, i, j])
 
     unrolled(BI, fields)
-
-    def viscosity(i):
-        rows = pl.ds(i + ETA_HALO - HALO - 1, 8, stride=BI)
-        own, beside = eta[rows, :], eta_side[rows, :]
-        for j in range(-1, BJ + 1):
-            col, at, outside = places(j)
-            near_side = jnp.where(outside, jnp.where(col < 0, col + 32, col - COLS + 32), 0)
-            eta_spread[i, j + 1] = jnp.where(outside, pick(beside, near_side), pick(own, at))
-
-    unrolled(BI + 2, viscosity)
 
 
 def store_state(state, c, i, values):
     values = [turn(values[BJ - 1], 1, 1)] + values + [turn(values[0], -1, 1)]
     for j, value in enumerate(values):
         state[c, i + 1, j] = value
-
-    def before(i):
+    if isinstance(i, int):
         for j, value in enumerate(values):
-            state[c, 0, j] = turn(value, 1, 0)
-
-    def after(i):
-        for j, value in enumerate(values):
-            state[c, BI + 1, j] = turn(value, -1, 0)
-
-    return before, after
-
-
-def wrap_rows(state):
-    for c in range(2):
-        for j in range(BJ + 2):
-            state[c, 0, j] = turn(state[c, BI, j], 1, 0)
-            state[c, BI + 1, j] = turn(state[c, 1, j], -1, 0)
+            if i == 0:
+                state[c, BI + 1, j] = turn(value, -1, 0)
+            else:
+                state[c, 0, j] = turn(value, 1, 0)
 
 
 def coefficients(spread, eta_spread, coef, weight, source, state, gx, gy, nx, ny):
@@ -157,8 +175,8 @@
             react = spread[3, i, j] + DRAG
             me, mw, mn, ms = m + e, m + w, m + n, m + s
             along, across = me + mw, mn + ms
-            w1 = jnp.where(inside, OMEGA / (2.0 * along + 0.5 * across + react), 0.0)
-            w2 = jnp.where(inside, OMEGA / (0.5 * along + 2.0 * across + react), 0.0)
+            w1 = jnp.where(inside, 1.0 / (2.0 * along + 0.5 * across + react), 0.0)
+            w2 = jnp.where(inside, 1.0 / (0.5 * along + 2.0 * across + react), 0.0)
             a1, b1, q1 = 2.0 * w1, 0.5 * w1, 0.25 * w1
             a2, b2, q2 = 2.0 * w2, 0.5 * w2, 0.25 * w2
             coef[0, i, j] = a1 * me
@@ -179,6 +197,7 @@
             coef[13, i, j] = bs + qe
             coef[14, i, j] = bn + qw
             coef[15, i, j] = bs + qw
+            w1, w2 = OMEGA * w1, OMEGA * w2
             noise = spread[4, i, j]
             weight[0, i, j] = w1 * noise
             weight[1, i, j] = w2 * noise
@@ -186,16 +205,15 @@
             f1, f2 = w1 * (spread[1, i, j] * probe), w2 * (spread[2, i, j] * probe)
             source[0, i, j] = f1
             source[1, i, j] = f2
-            first.append(f1)
-            second.append(f2)
+            first.append(SERIES[-1] * f1)
+            second.append(SERIES[-1] * f2)
         store_state(state, 0, i, first)
         store_state(state, 1, i, second)
 
-    unrolled(BI, row)
-    wrap_rows(state)
-
-
-def sweep(old, new, coef, source):
+    ends_first(row)
+
+
+def sweep(old, new, coef, source, factor):
     def row(i):
         first, second = [], []
         for j in range(BJ):
@@ -205,14 +223,14 @@
 
             k = [coef[n, i, j] for n in range(16)]
             first.append(
-                (0.4 * at(0, 0, 0) + source[0, i, j])
+                factor * source[0, i, j]
                 + (k[0] * at(0, 1, 0) + k[1] * at(0, -1, 0))
                 + (k[2] * at(0, 0, 1) + k[3] * at(0, 0, -1))
                 + (k[4] * at(1, 1, 1) - k[5] * at(1, 1, -1))
                 + (k[7] * at(1, -1, -1) - k[6] * at(1, -1, 1))
             )
             second.append(
-                (0.4 * at(1, 0, 0) + source[1, i, j])
+                factor * source[1, i, j]
                 + (k[8] * at(1, 1, 0) + k[9] * at(1, -1, 0))
                 + (k[10] * at(1, 0, 1) + k[11] * at(1, 0, -1))
                 + (k[12] * at(0, 1, 1) - k[13] * at(0, 1, -1))
@@ -221,17 +239,24 @@
         store_state(new, 0, i, first)
         store_state(new, 1, i, second)
 
-    unrolled(BI, row)
-    wrap_rows(new)
-
-
-def relax(state_a, state_b, coef, source):
-    def two(k, carry):
-        sweep(state_a, state_b, coef, source)
-        sweep(state_b, state_a, coef, source)
+    ends_first(row)
+
+
+def relax_twice(state_a, state_b, coef, weight, source):
+    def step(k, carry):
+        second = (k & 1) == 1
+        for n in range((SWEEPS - 1) // 2):
+            factor = jnp.where(second, SERIES[(SWEEPS - 1) // 2 - 1 - n], SERIES[SWEEPS - 2 - n])
+            old, new = (state_a, state_b) if n % 2 == 0 else (state_b, state_a)
+            sweep(old, new, coef, source, factor)
+
+        @pl.when(k == 1)
+        def _():
+            next_source(state_a, weight, source)
+
         return carry
 
-    lax.fori_loop(0, (SWEEPS - 1) // 2, two, 0)
+    lax.fori_loop(0, 4, step, 0)
 
 
 def next_source(state, weight, source):
@@ -240,10 +265,9 @@
             values = [weight[c, i, j] * state[c, i + 1, j + 1] for j in range(BJ)]
             for j in range(BJ):
                 source[c, i, j] = values[j]
-            store_state(state, c, i, values)
-
-    unrolled(BI, row)
-    wrap_rows(state)
+            store_state(state, c, i, [SERIES[-1] * value for value in values])
+
+    ends_first(row)
 
 
 def gather_images(state, spread, natural):
@@ -291,7 +315,7 @@
     vel, fric, mask, side, eta_side, spread, eta_spread, coef, weight, source, state_a, state_b,
     natural, other_probes, message, inbox_a, inbox_b,
     in_sem, halo_send, halo_recv, eta_send, eta_recv, pair_send, pair_recv,
-    a_send, a_recv, b_send, b_recv,
+    a_send, a_recv, b_send, b_recv, near_a, near_b,
 ):
     half, gx, gy = lax.axis_index("probe"), lax.axis_index("gx"), lax.axis_index("gy")
     group_a, group_b = nx_devices, 2 * ny_devices
@@ -347,23 +371,47 @@
     def at_b(t):
         return {"probe": lax.rem(t, 2), "gy": lax.div(t, 2)}
 
+    def along_x(step):
+        return {"gx": lax.rem(gx + step + nx_devices, nx_devices)}
+
+    def along_y(step):
+        return {"gy": lax.rem(gy + step + ny_devices, ny_devices)}
+
+    partner = {"probe": 1 - half}
+
+    def signal(semaphore, to):
+        pl.semaphore_signal(semaphore, inc=1, device_id=to, device_id_type=MESH)
+
     barrier = pltpu.get_barrier_semaphore()
     for dx, dy in AROUND:
 
         @pl.when(exists(dx, dy))
         def _():
-            pl.semaphore_signal(barrier, inc=1, device_id={"gx": gx + dx, "gy": gy + dy}, device_id_type=MESH)
-
-    def greet_a(k, carry):
-        pl.semaphore_signal(barrier, inc=1, device_id={"gx": lax.rem(gx + k, group_a)}, device_id_type=MESH)
-        return carry
-
-    def greet_b(k, carry):
-        pl.semaphore_signal(barrier, inc=1, device_id=at_b(lax.rem(me_b + k, group_b)), device_id_type=MESH)
-        return carry
-
-    lax.fori_loop(1, group_a, greet_a, 0)
-    lax.fori_loop(1, group_b, greet_b, 0)
+            signal(barrier, {"gx": gx + dx, "gy": gy + dy})
+
+    first_x, last_x = gx == 0, gx == nx_devices - 1
+    first_y, last_y = gy == 0, gy == ny_devices - 1
+
+    @pl.when(first_x | last_x)
+    def _():
+        signal(barrier, {"gx": nx_devices - 1 - gx})
+
+    @pl.when(first_y | last_y)
+    def _():
+        signal(barrier, {"gy": ny_devices - 1 - gy})
+
+    signal(barrier, partner)
+
+    def relay(stage):
+        for step in (-(2**stage), 2**stage):
+            signal(near_a.at[stage], along_x(step))
+            if stage < 2:
+                signal(near_b.at[stage], along_y(step))
+        signal(near_b.at[stage], partner)
+
+    def hear(stage):
+        pl.semaphore_wait(near_a.at[stage], 2)
+        pl.semaphore_wait(near_b.at[stage], 3 if stage < 2 else 1)
 
     for load in loads:
         load.wait()
@@ -373,9 +421,8 @@
     ext[6, own_rows, :] = coupling
     pack_strips(ext, eta, left, right, eta_left, eta_right)
 
-    tall = jnp.where((gx > 0) & (gx < nx_devices - 1), 3, jnp.where(nx_devices > 1, 2, 1))
-    long = jnp.where((gy > 0) & (gy < ny_devices - 1), 3, jnp.where(ny_devices > 1, 2, 1))
-    pl.semaphore_wait(barrier, tall * long - 1 + (group_a - 1) + (group_b - 1))
+    edge_x, edge_y = (first_x | last_x).astype(jnp.int32), (first_y | last_y).astype(jnp.int32)
+    pl.semaphore_wait(barrier, (3 - edge_x) * (3 - edge_y) + edge_x + edge_y)
 
     def halo_copies(n):
         dx, dy = AROUND[n]
@@ -405,6 +452,8 @@
             for copy in halo_copies(n):
                 copy.start()
 
+    relay(0)
+
     probe_copy = pltpu.make_async_remote_copy(
         src_ref=ext.at[0:HALF, own_rows, :], dst_ref=other_probes,
         send_sem=pair_send.at[0], recv_sem=pair_recv.at[0], device_id={"probe": 1 - half}, device_id_type=MESH,
@@ -414,41 +463,50 @@
         send_sem=pair_send.at[1], recv_sem=pair_recv.at[1], device_id={"probe": 1 - half}, device_id_type=MESH,
     )
 
+    def await_halos(directions):
+        for n in directions:
+            dx, dy = AROUND[n]
+
+            @pl.when(exists(-dx, -dy))
+            def _():
+                for copy in halo_copies(n):
+                    copy.wait_recv()
+
+    await_halos((0, 1))
+    relayout_own(ext, eta, spread, eta_spread)
+    await_halos(range(2, 8))
+
     @pl.when(half == 1)
     def _():
         probe_copy.start()
 
-    for n, (dx, dy) in enumerate(AROUND):
-
-        @pl.when(exists(-dx, -dy))
-        def _():
-            for copy in halo_copies(n):
-                copy.wait_recv()
-
-    relayout(ext, west, east, eta, eta_west, eta_east, side, eta_side, spread, eta_spread)
+    hear(0)
+    relay(1)
+    relayout_sides(west, east, eta_west, eta_east, side, eta_side, spread, eta_spread)
     coefficients(
         spread, eta_spread, coef, weight, source, state_a, gx, gy, nx_devices * ROWS, ny_devices * COLS
     )
-    relax(state_a, state_b, coef, source)
-    next_source(state_a, weight, source)
-    relax(state_a, state_b, coef, source)
+    hear(1)
+    relay(2)
+    relax_twice(state_a, state_b, coef, weight, source)
     gather_images(state_a, spread, natural)
 
     @pl.when(half == 0)
     def _():
         image_copy.start()
 
+    hear(2)
     own = products(ext, HALO, natural, HALO)
 
     @pl.when(half == 0)
     def _():
         probe_copy.wait_recv()
         cross = products(other_probes, 0, natural, HALO)
-        message[0] = jnp.broadcast_to(own + turn(cross, 16, 1), (8, 128))
+        message[0] = own + turn(cross, 16, 1)
 
     @pl.when(half == 1)
     def _():
-        message[0] = jnp.broadcast_to(turn(own, 32, 1), (8, 128))
+        message[0] = turn(own, 32, 1)
 
     def reduce(phase, inbox, me, count, sends, recvs, place):
         def copy_to(k):
@@ -477,6 +535,8 @@
 
         lax.fori_loop(1, count, send, 0)
         inbox[me] = message[phase]
+        if phase == 0:
+            images[...] = natural[:, own_rows, :]
         lax.fori_loop(1, count, receive, 0)
         total = inbox[0]
         for k in range(1, count):
@@ -486,8 +546,7 @@
     total, done_a = reduce(0, inbox_a, gx, group_a, a_send, a_recv, lambda t: {"gx": t})
     message[1] = total
     total, done_b = reduce(1, inbox_b, me_b, group_b, b_send, b_recv, at_b)
-    gram[...] = total * (1.0 / (nx_devices * ROWS * ny_devices * COLS))
-    images[...] = natural[:, own_rows, :]
+    gram[...] = jnp.broadcast_to(total * (1.0 / (nx_devices * ROWS * ny_devices * COLS)), (8, 128))
 
     for n, (dx, dy) in enumerate(AROUND):
 
@@ -509,51 +568,44 @@
         image_copy.wait_recv()
 
 
-def last_kernel(sums, images, other_images, images_out, factor, gram):
+def last_kernel(sums, images, other_images, images_out, factor, gram, factor_here, gram_here, sems):
     half = lax.axis_index("probe")
+    images_copy = pltpu.make_async_copy(images, images_out, sems.at[0])
+    images_copy.start()
+
+    lane, sub = lanes(), sublanes()
+    low_row, low_col = sub < HALF, lane < HALF
+    a, b = sub & (HALF - 1), lane & (HALF - 1)
+    at = jnp.where(low_row == low_col, HALF * a + b, jnp.where(low_col, HALF * a + b, HALF * b + a))
+    at = at + jnp.where(low_row == low_col, jnp.where(low_row, 0, 2 * HALF * HALF), HALF * HALF)
+    row = sums[...]
+    full = pick(row, jnp.where(lane < 2 * HALF, at, 0))
+    gram_here[...] = full[:, : 2 * HALF]
+    gram_copy = pltpu.make_async_copy(gram_here, gram, sems.at[1])
+    gram_copy.start()
 
     def entry(i, j):
-        i, j = max(i, j), min(i, j)
-        if i < HALF:
-            return sums[0, 4 * i + j]
-        if j < HALF:
-            return sums[0, 16 + 4 * (i - HALF) + j]
-        return sums[0, 32 + 4 * (i - HALF) + j - HALF]
+        k = HALF * (i % HALF) + j % HALF
+        if (i < HALF) == (j < HALF):
+            return jnp.broadcast_to(row[:, (k if i < HALF else k + 32) :][:, :1], (8, 128))
+        return jnp.broadcast_to(row[:, k + 16 :][:, :1], (8, 128))
 
     count = 2 * HALF
-    g = {(i, j): jnp.full((8, 128), entry(i, j), F32) for i in range(count) for j in range(i + 1)}
-    for i in range(count):
-        for j in range(i):
-            if (i < HALF) == (j < HALF):
-                k = 4 * (j % HALF) + i % HALF + (0 if i < HALF else 32)
-                g[i, j] = 0.5 * (g[i, j] + jnp.full((8, 128), sums[0, k], F32))
-    lane, sub = lanes(), sublanes()
-    out = jnp.zeros((8, 128), F32)
-    for i in range(count):
-        row = jnp.zeros((8, 128), F32)
-        for j in range(count):
-            a, b = i % HALF, j % HALF
-            if (i < HALF) == (j < HALF):
-                value = sums[0, 4 * a + b + (0 if i < HALF else 32)]
-            else:
-                value = entry(i, j)
-            row = jnp.where(lane == j, value, row)
-        out = jnp.where(sub == i, row, out)
-    gram[...] = out[:, :count]
-
     low, inverse = {}, {}
     for j in range(count):
         for i in range(j, count):
-            value = g[i, j]
+            value = entry(i, j)
+            if i != j and (i < HALF) == (j < HALF):
+                value = 0.5 * (value + entry(j, i))
             for k in range(j):
                 value = value - low[i, k] * low[j, k]
             if i == j:
-                root = jnp.sqrt(value)
-                inverse[j] = 1.0 / root
+                guess = lax.rsqrt(value)
+                inverse[j] = guess * (1.5 - 0.5 * value * guess * guess)
             else:
                 low[i, j] = value * inverse[j]
 
-    def solve(sources, out_rows):
+    def solve(sources):
         def part(k):
             rows = pl.ds(8 * k, 8)
             done = []
@@ -564,19 +616,23 @@
                 value = value * inverse[i]
                 done.append(value)
                 if i >= len(sources) - HALF:
-                    factor[i - len(sources) + HALF, rows, :] = value
+                    factor_here[i - len(sources) + HALF, rows, :] = value
 
         unrolled(ROWS // 8, part)
 
-    images_out[...] = images[...]
-
     @pl.when(half == 0)
     def _():
-        solve([(images, p) for p in range(HALF)], 0)
+        solve([(images, p) for p in range(HALF)])
 
     @pl.when(half == 1)
     def _():
-        solve([(other_images, p) for p in range(HALF)] + [(images, p) for p in range(HALF)], HALF)
+        solve([(other_images, p) for p in range(HALF)] + [(images, p) for p in range(HALF)])
+
+    factor_copy = pltpu.make_async_copy(factor_here, factor, sems.at[2])
+    factor_copy.start()
+    images_copy.wait()
+    gram_copy.wait()
+    factor_copy.wait()
 
 
 def body(probes, velocity, eta, friction, noise, ice):
@@ -600,19 +656,23 @@
             vmem(2, EXT, 128), vmem(ROWS + 2 * ETA_HALO, 128),
             vmem(5, *grid), vmem(*padded), vmem(16, *grid), vmem(2, *grid), vmem(2, *grid),
             vmem(2, *padded), vmem(2, *padded),
-            vmem(HALF, EXT, 128), vmem(HALF, ROWS, COLS), vmem(2, 8, 128), vmem(group_a, 8, 128), vmem(group_b, 8, 128),
+            vmem(HALF, EXT, 128), vmem(HALF, ROWS, COLS), vmem(2, 1, 128), vmem(group_a, 1, 128), vmem(group_b, 1, 128),
             dma(6), dma(8), dma(8), dma(8), dma(8), dma(2), dma(2),
             dma(group_a), dma(group_a), dma(group_b), dma(group_b),
+            pltpu.SemaphoreType.REGULAR((3,)), pltpu.SemaphoreType.REGULAR((3,)),
         ],
         compiler_params=pltpu.CompilerParams(
             collective_id=0, has_side_effects=True, vmem_limit_bytes=32 * 1024 * 1024
         ),
-    )(probes, velocity, eta, friction, noise, ice)
+    )(*[pltpu.with_memory_space_constraint(x, pltpu.HBM) for x in (probes, velocity, eta, friction, noise, ice)])
+    square = (2 * HALF, 2 * HALF)
     return pl.pallas_call(
         last_kernel,
-        out_shape=(tile, tile, jax.ShapeDtypeStruct((2 * HALF, 2 * HALF), F32)),
-        in_specs=[pl.BlockSpec(memory_space=pltpu.SMEM), whole, whole],
-        out_specs=(whole, whole, whole),
+        out_shape=(tile, tile, jax.ShapeDtypeStruct(square, F32)),
+        in_specs=[whole, whole, whole],
+        out_specs=(pl.BlockSpec(memory_space=pl.ANY),) * 3,
+        scratch_shapes=[vmem(HALF, ROWS, COLS), vmem(*square), dma(3)],
+        compiler_params=pltpu.CompilerParams(vmem_limit_bytes=16 * 1024 * 1024),
     )(sums, images, other_images)
 
 

time: 46.3 us -> 34.7 us (0.75)
  local copies, waits for them, and re-layouts: 6.65 us -> 0 us
  Pallas kernels: 38.6 us -> 34 us
    unnamed x18 -> x0, local copies, waits for them, and re-layouts: 6.65 us -> none
    pallas_call x1, Pallas kernels: 36.7 us -> 33.1 us  [body(): pl.pallas_call(functools.partial(main_kernel, nx_devices, ny_devices), ou...]
    pallas_call x1, Pallas kernels: 1.85 us -> 0.87 us  [body(): pl.pallas_call(last_kernel, out_shape=(tile, tile, jax.ShapeDtypeStruct(s...]
where the time goes in v2:
time: 34.7 us; the launch traced here: 34.6 us
  Pallas kernels  34 us (98%)
  between operations  0.64 us (2%)
    pallas_call x1, Pallas kernels, body(): pl.pallas_call(functools.partial(main_kernel, nx_devices, ny_devices), ou...  33.1 us
    pallas_call x1, Pallas kernels, body(): pl.pallas_call(last_kernel, out_shape=(tile, tile, jax.ShapeDtypeStruct(s...  0.87 us

profile of v2, /device:TPU:1, one launch (start us, length us, event | category | flops | bytes accessed | tf_op | source)
XLA Modules:
  0.0 34.6 jit_solution(2798601466642040350)
XLA Ops:
  0.6 33.1 %shard_map.85 = (f32[4,64,128]{2,1,0:T(8,128)S(1)}, f32[4,64,128]{2,1,0:T(8,128)S(1)}, f32[8,128]{1,0:T(8,128)S(1)}) custom-call(f32[4,64,128]{2,1,0:T(8,128)} %probes.1, f32[2,64,128]{2,1,0:T(8,128)} %velocity.1, f32[64,128]{1,0:T(8,128)} %eta_in.1, f32[64,128]{1,0:T(8,128)} %friction.1, f32[64,128]{1,0:T(8,128)} %noise.1, s32[64,128]{1,0:T(8,128)} %ice.1), custom_call_target="tpu_custom_call" | custom-call | tf_op jit(solution)/shard_map/pallas_call | solution.py:647
  33.7 0.9 %shard_map.86 = (f32[4,64,128]{2,1,0:T(8,128)}, f32[4,64,128]{2,1,0:T(8,128)}, f32[8,8]{1,0:T(8,128)}) custom-call(f32[8,128]{1,0:T(8,128)S(1)} %get-tuple-element.6.sums, f32[4,64,128]{2,1,0:T(8,128)S(1)} %get-tuple-element.7.images, f32[4,64,128]{2,1,0:T(8,128)S(1)} %get-tuple-element.8.other_images), custom_call_target="tpu_custom_call" | custom-call | tf_op jit(solution)/shard_map/pallas_call | solution.py:669

commit v3 on v2

--- a/solution.py
+++ b/solution.py
@@ -159,6 +159,12 @@
                 state[c, 0, j] = turn(value, 1, 0)
 
 
+def recip(x):
+    y = pl.reciprocal(x, approx=True)
+    y = y * (2.0 - x * y)
+    return y * (2.0 - x * y)
+
+
 def coefficients(spread, eta_spread, coef, weight, source, state, gx, gy, nx, ny):
     lane, sub = lanes(), sublanes()
 
@@ -175,8 +181,8 @@
             react = spread[3, i, j] + DRAG
             me, mw, mn, ms = m + e, m + w, m + n, m + s
             along, across = me + mw, mn + ms
-            w1 = jnp.where(inside, 1.0 / (2.0 * along + 0.5 * across + react), 0.0)
-            w2 = jnp.where(inside, 1.0 / (0.5 * along + 2.0 * across + react), 0.0)
+            w1 = jnp.where(inside, recip(2.0 * along + 0.5 * across + react), 0.0)
+            w2 = jnp.where(inside, recip(0.5 * along + 2.0 * across + react), 0.0)
             a1, b1, q1 = 2.0 * w1, 0.5 * w1, 0.25 * w1
             a2, b2, q2 = 2.0 * w2, 0.5 * w2, 0.25 * w2
             coef[0, i, j] = a1 * me
@@ -242,21 +248,21 @@
     ends_first(row)
 
 
-def relax_twice(state_a, state_b, coef, weight, source):
+def relax_twice(state_a, state_b, coef, source, between):
+
     def step(k, carry):
-        second = (k & 1) == 1
-        for n in range((SWEEPS - 1) // 2):
-            factor = jnp.where(second, SERIES[(SWEEPS - 1) // 2 - 1 - n], SERIES[SWEEPS - 2 - n])
+        for n in range(SWEEPS - 1):
+            factor = SERIES[SWEEPS - 2 - n]
             old, new = (state_a, state_b) if n % 2 == 0 else (state_b, state_a)
             sweep(old, new, coef, source, factor)
 
-        @pl.when(k == 1)
+        @pl.when(k == 0)
         def _():
-            next_source(state_a, weight, source)
+            between()
 
         return carry
 
-    lax.fori_loop(0, 4, step, 0)
+    lax.fori_loop(0, 2, step, 0)
 
 
 def next_source(state, weight, source):
@@ -313,13 +319,11 @@
     images, other_images, gram,
     ext, west, east, left, right, eta, eta_west, eta_east, eta_left, eta_right,
     vel, fric, mask, side, eta_side, spread, eta_spread, coef, weight, source, state_a, state_b,
-    natural, other_probes, message, inbox_a, inbox_b,
+    natural, other_probes, message, inbox,
     in_sem, halo_send, halo_recv, eta_send, eta_recv, pair_send, pair_recv,
-    a_send, a_recv, b_send, b_recv, near_a, near_b,
+    sum_send, sum_recv, heard,
 ):
     half, gx, gy = lax.axis_index("probe"), lax.axis_index("gx"), lax.axis_index("gy")
-    group_a, group_b = nx_devices, 2 * ny_devices
-    me_b = gy * 2 + half
     own_rows = slice(HALO, HALO + ROWS)
 
     loads = [
@@ -368,14 +372,8 @@
         x, y = gx + dx, gy + dy
         return (x >= 0) & (x < nx_devices) & (y >= 0) & (y < ny_devices)
 
-    def at_b(t):
-        return {"probe": lax.rem(t, 2), "gy": lax.div(t, 2)}
-
-    def along_x(step):
-        return {"gx": lax.rem(gx + step + nx_devices, nx_devices)}
-
-    def along_y(step):
-        return {"gy": lax.rem(gy + step + ny_devices, ny_devices)}
+    def away(dx, dy):
+        return {"gx": lax.rem(gx + dx + nx_devices, nx_devices), "gy": lax.rem(gy + dy + ny_devices, ny_devices)}
 
     partner = {"probe": 1 - half}
 
@@ -384,34 +382,18 @@
 
     barrier = pltpu.get_barrier_semaphore()
     for dx, dy in AROUND:
-
-        @pl.when(exists(dx, dy))
-        def _():
-            signal(barrier, {"gx": gx + dx, "gy": gy + dy})
-
-    first_x, last_x = gx == 0, gx == nx_devices - 1
-    first_y, last_y = gy == 0, gy == ny_devices - 1
-
-    @pl.when(first_x | last_x)
-    def _():
-        signal(barrier, {"gx": nx_devices - 1 - gx})
-
-    @pl.when(first_y | last_y)
-    def _():
-        signal(barrier, {"gy": ny_devices - 1 - gy})
-
+        signal(barrier, away(dx, dy))
     signal(barrier, partner)
 
+    relays = (AROUND, [(2 * dx, 2 * dy) for dx, dy in AROUND], [(-4, 0), (4, 0)], [])
+
     def relay(stage):
-        for step in (-(2**stage), 2**stage):
-            signal(near_a.at[stage], along_x(step))
-            if stage < 2:
-                signal(near_b.at[stage], along_y(step))
-        signal(near_b.at[stage], partner)
+        for dx, dy in relays[stage]:
+            signal(heard.at[stage], away(dx, dy))
+        signal(heard.at[stage], partner)
 
     def hear(stage):
-        pl.semaphore_wait(near_a.at[stage], 2)
-        pl.semaphore_wait(near_b.at[stage], 3 if stage < 2 else 1)
+        pl.semaphore_wait(heard.at[stage], len(relays[stage]) + 1)
 
     for load in loads:
         load.wait()
@@ -421,8 +403,7 @@
     ext[6, own_rows, :] = coupling
     pack_strips(ext, eta, left, right, eta_left, eta_right)
 
-    edge_x, edge_y = (first_x | last_x).astype(jnp.int32), (first_y | last_y).astype(jnp.int32)
-    pl.semaphore_wait(barrier, (3 - edge_x) * (3 - edge_y) + edge_x + edge_y)
+    pl.semaphore_wait(barrier, len(AROUND) + 1)
 
     def halo_copies(n):
         dx, dy = AROUND[n]
@@ -445,7 +426,7 @@
             for (src, dst), sends, recvs in ((main, halo_send, halo_recv), (more, eta_send, eta_recv))
         ]
 
-    for n, (dx, dy) in enumerate(AROUND):
+    for n, (dx, dy) in reversed(list(enumerate(AROUND))):
 
         @pl.when(exists(dx, dy))
         def _():
@@ -474,28 +455,34 @@
 
     await_halos((0, 1))
     relayout_own(ext, eta, spread, eta_spread)
-    await_halos(range(2, 8))
-
-    @pl.when(half == 1)
-    def _():
-        probe_copy.start()
-
     hear(0)
     relay(1)
+    await_halos(range(2, 8))
+
+    @pl.when(half == 1)
+    def _():
+        probe_copy.start()
+
     relayout_sides(west, east, eta_west, eta_east, side, eta_side, spread, eta_spread)
     coefficients(
         spread, eta_spread, coef, weight, source, state_a, gx, gy, nx_devices * ROWS, ny_devices * COLS
     )
     hear(1)
     relay(2)
-    relax_twice(state_a, state_b, coef, weight, source)
+
+    def between():
+        next_source(state_a, weight, source)
+        hear(2)
+        relay(3)
+
+    relax_twice(state_a, state_b, coef, source, between)
     gather_images(state_a, spread, natural)
 
     @pl.when(half == 0)
     def _():
         image_copy.start()
 
-    hear(2)
+    hear(3)
     own = products(ext, HALO, natural, HALO)
 
     @pl.when(half == 0)
@@ -508,44 +495,44 @@
     def _():
         message[0] = turn(own, 32, 1)
 
-    def reduce(phase, inbox, me, count, sends, recvs, place):
-        def copy_to(k):
-            return pltpu.make_async_remote_copy(
-                src_ref=message.at[phase], dst_ref=inbox.at[me], send_sem=sends.at[k], recv_sem=recvs.at[me],
-                device_id=place(lax.rem(me + k, count)), device_id_type=MESH,
-            )
-
-        def copy_from(k):
-            return pltpu.make_async_remote_copy(
-                src_ref=message.at[phase], dst_ref=inbox.at[k], send_sem=sends.at[0], recv_sem=recvs.at[k],
-                device_id=place(k), device_id_type=MESH,
-            )
-
-        def send(k, carry):
-            copy_to(k).start()
-            return carry
-
-        def receive(k, carry):
-            copy_from(lax.rem(me + k, count)).wait_recv()
-            return carry
-
-        def sent(k, carry):
-            copy_to(k).wait_send()
-            return carry
-
-        lax.fori_loop(1, count, send, 0)
-        inbox[me] = message[phase]
-        if phase == 0:
-            images[...] = natural[:, own_rows, :]
-        lax.fori_loop(1, count, receive, 0)
-        total = inbox[0]
-        for k in range(1, count):
-            total = total + inbox[k]
-        return total, lambda: lax.fori_loop(1, count, sent, 0)
-
-    total, done_a = reduce(0, inbox_a, gx, group_a, a_send, a_recv, lambda t: {"gx": t})
-    message[1] = total
-    total, done_b = reduce(1, inbox_b, me_b, group_b, b_send, b_recv, at_b)
+    me = (gx * ny_devices + gy) * 2 + half
+    everyone = 2 * nx_devices * ny_devices
+
+    def sum_copy(dx, dy, dp, to_all):
+        to = {
+            "gx": lax.rem(gx + dx, nx_devices),
+            "gy": lax.rem(gy + dy, ny_devices),
+            "probe": lax.rem(half + dp, 2),
+        }
+        rows = everyone - 1 if to_all else 1
+        src = inbox.at[0:rows] if to_all else message
+        dst = inbox.at[0:rows] if to_all else inbox.at[pl.ds(me, 1)]
+        return pltpu.make_async_remote_copy(
+            src_ref=src, dst_ref=dst, send_sem=sum_send, recv_sem=sum_recv, device_id=to, device_id_type=MESH
+        )
+
+    y_order = (4, 3, 5, 2, 6, 1, 7, 0)
+
+    def send_sums(k, carry):
+        step = lax.div(k + 1, 2)
+        dx = lax.rem(nx_devices // 2 + nx_devices + jnp.where(lax.rem(k, 2) == 0, step, -step), nx_devices)
+        for dy in y_order:
+            for dp in (1, 0):
+                if dy == 0 and dp == 0:
+
+                    @pl.when(dx != 0)
+                    def _():
+                        sum_copy(dx, dy, dp, False).start()
+                else:
+                    sum_copy(dx, dy, dp, False).start()
+        return carry
+
+    lax.fori_loop(0, nx_devices, send_sums, 0)
+    inbox[pl.ds(me, 1)] = message[...]
+    images[...] = natural[:, own_rows, :]
+    all_sums = sum_copy(1, 0, 0, True)
+    all_sums.wait_recv()
+    total = jnp.sum(jnp.sum(inbox[...].reshape(everyone // 8, 8, 128), axis=0), axis=0, keepdims=True)
     gram[...] = jnp.broadcast_to(total * (1.0 / (nx_devices * ROWS * ny_devices * COLS)), (8, 128))
 
     for n, (dx, dy) in enumerate(AROUND):
@@ -555,8 +542,7 @@
             for copy in halo_copies(n):
                 copy.wait_send()
 
-    done_a()
-    done_b()
+    all_sums.wait_send()
 
     @pl.when(half == 0)
     def _():
@@ -643,7 +629,6 @@
     padded = (BI + 2, BJ + 2, 8, 128)
     whole = pl.BlockSpec(memory_space=pltpu.VMEM)
     tile = jax.ShapeDtypeStruct((HALF, ROWS, COLS), F32)
-    group_a, group_b = nx_devices, 2 * ny_devices
     images, other_images, sums = pl.pallas_call(
         functools.partial(main_kernel, nx_devices, ny_devices),
         out_shape=(tile, tile, jax.ShapeDtypeStruct((8, 128), F32)),
@@ -656,10 +641,10 @@
             vmem(2, EXT, 128), vmem(ROWS + 2 * ETA_HALO, 128),
             vmem(5, *grid), vmem(*padded), vmem(16, *grid), vmem(2, *grid), vmem(2, *grid),
             vmem(2, *padded), vmem(2, *padded),
-            vmem(HALF, EXT, 128), vmem(HALF, ROWS, COLS), vmem(2, 1, 128), vmem(group_a, 1, 128), vmem(group_b, 1, 128),
+            vmem(HALF, EXT, 128), vmem(HALF, ROWS, COLS), vmem(1, 1, 128), vmem(2 * nx_devices * ny_devices, 1, 128),
             dma(6), dma(8), dma(8), dma(8), dma(8), dma(2), dma(2),
-            dma(group_a), dma(group_a), dma(group_b), dma(group_b),
-            pltpu.SemaphoreType.REGULAR((3,)), pltpu.SemaphoreType.REGULAR((3,)),
+            pltpu.SemaphoreType.DMA, pltpu.SemaphoreType.DMA,
+            pltpu.SemaphoreType.REGULAR((4,)),
         ],
         compiler_params=pltpu.CompilerParams(
             collective_id=0, has_side_effects=True, vmem_limit_bytes=32 * 1024 * 1024

time: 34.7 us -> 33.5 us (0.965)
  Pallas kernels: 34 us -> 32.8 us
    pallas_call x1, Pallas kernels: 33.1 us -> 31.9 us  [body(): pl.pallas_call(functools.partial(main_kernel, nx_devices, ny_devices), ou...]
where the time goes in v3:
time: 33.5 us; the launch traced here: 33.4 us
  Pallas kernels  32.8 us (98%)
  between operations  0.64 us (2%)
    pallas_call x1, Pallas kernels, body(): pl.pallas_call(functools.partial(main_kernel, nx_devices, ny_devices), ou...  31.9 us
    pallas_call x1, Pallas kernels, body(): pl.pallas_call(last_kernel, out_shape=(tile, tile, jax.ShapeDtypeStruct(s...  0.87 us

profile of v3, /device:TPU:1, one launch (start us, length us, event | category | flops | bytes accessed | tf_op | source)
XLA Modules:
  0.0 33.4 jit_solution(16270182426804392998)
XLA Ops:
  0.6 31.9 %shard_map.85 = (f32[4,64,128]{2,1,0:T(8,128)S(1)}, f32[4,64,128]{2,1,0:T(8,128)S(1)}, f32[8,128]{1,0:T(8,128)S(1)}) custom-call(f32[4,64,128]{2,1,0:T(8,128)} %probes.1, f32[2,64,128]{2,1,0:T(8,128)} %velocity.1, f32[64,128]{1,0:T(8,128)} %eta_in.1, f32[64,128]{1,0:T(8,128)} %friction.1, f32[64,128]{1,0:T(8,128)} %noise.1, s32[64,128]{1,0:T(8,128)} %ice.1), custom_call_target="tpu_custom_call" | custom-call | tf_op jit(solution)/shard_map/pallas_call | solution.py:632
  32.6 0.9 %shard_map.86 = (f32[4,64,128]{2,1,0:T(8,128)}, f32[4,64,128]{2,1,0:T(8,128)}, f32[8,8]{1,0:T(8,128)}) custom-call(f32[8,128]{1,0:T(8,128)S(1)} %get-tuple-element.6.sums, f32[4,64,128]{2,1,0:T(8,128)S(1)} %get-tuple-element.7.images, f32[4,64,128]{2,1,0:T(8,128)S(1)} %get-tuple-element.8.other_images), custom_call_target="tpu_custom_call" | custom-call | tf_op jit(solution)/shard_map/pallas_call | solution.py:654

commit v4 on v3

--- a/solution.py
+++ b/solution.py
@@ -18,6 +18,7 @@
 HALO = 2 * (SWEEPS - 1)
 BI, BJ = (ROWS + 2 * HALO) // 8, (COLS + 2 * HALO) // 32
 EXT = ROWS + 2 * HALO
+ROOM = 16
 ETA_HALO = 24
 MESH = pl.DeviceIdType.MESH
 F32 = jnp.float32
@@ -114,8 +115,8 @@
     group = lane >> 5
     wide = lax.broadcasted_iota(jnp.int32, (EXT, COLS), 1)
     w, e = west[...], east[...]
-    side[0] = jnp.where(wide < 64, w, turn(e, 64, 1))
-    side[1] = jnp.where(wide < 64, turn(w, 64, 1), e)
+    side[0, 0:EXT, :] = jnp.where(wide < 64, w, turn(e, 64, 1))
+    side[1, 0:EXT, :] = jnp.where(wide < 64, turn(w, 64, 1), e)
     for k in range(14):
         own_row = 8 * k - ETA_HALO
         slot = 0 if own_row < 0 else (1 if own_row < ROWS else 2)
@@ -635,13 +636,13 @@
         in_specs=[pl.BlockSpec(memory_space=pl.ANY)] * 6,
         out_specs=(whole, whole, whole),
         scratch_shapes=[
-            vmem(8, EXT, 128), vmem(EXT, 128), vmem(EXT, 128), vmem(ROWS, 128), vmem(ROWS, 128),
-            vmem(ROWS + 2 * ETA_HALO, 128), vmem(3, 16, 128), vmem(3, 16, 128), vmem(16, 128), vmem(16, 128),
+            vmem(8, EXT + ROOM, 128), vmem(EXT, 128), vmem(EXT, 128), vmem(ROWS, 128), vmem(ROWS, 128),
+            vmem(ROWS + 2 * ETA_HALO + ROOM, 128), vmem(3, 16, 128), vmem(3, 16, 128), vmem(16, 128), vmem(16, 128),
             vmem(2, ROWS, COLS), vmem(ROWS, COLS), pltpu.VMEM((ROWS, COLS), jnp.int32),
-            vmem(2, EXT, 128), vmem(ROWS + 2 * ETA_HALO, 128),
+            vmem(2, EXT + ROOM, 128), vmem(ROWS + 2 * ETA_HALO + ROOM, 128),
             vmem(5, *grid), vmem(*padded), vmem(16, *grid), vmem(2, *grid), vmem(2, *grid),
             vmem(2, *padded), vmem(2, *padded),
-            vmem(HALF, EXT, 128), vmem(HALF, ROWS, COLS), vmem(1, 1, 128), vmem(2 * nx_devices * ny_devices, 1, 128),
+            vmem(HALF, EXT + ROOM, 128), vmem(HALF, ROWS, COLS), vmem(1, 1, 128), vmem(2 * nx_devices * ny_devices, 1, 128),
             dma(6), dma(8), dma(8), dma(8), dma(8), dma(2), dma(2),
             pltpu.SemaphoreType.DMA, pltpu.SemaphoreType.DMA,
             pltpu.SemaphoreType.REGULAR((4,)),

time: 33.5 us -> 33.5 us (level)
  no operation moved by 1% of the time
where the time goes in v4:
time: 33.5 us; the launch traced here: 33.4 us
  Pallas kernels  32.8 us (98%)
  between operations  0.64 us (2%)
    pallas_call x1, Pallas kernels, body(): pl.pallas_call(functools.partial(main_kernel, nx_devices, ny_devices), ou...  31.9 us
    pallas_call x1, Pallas kernels, body(): pl.pallas_call(last_kernel, out_shape=(tile, tile, jax.ShapeDtypeStruct(s...  0.87 us

profile of v4, /device:TPU:1, one launch (start us, length us, event | category | flops | bytes accessed | tf_op | source)
XLA Modules:
  0.0 33.4 jit_solution(3545694663911800138)
XLA Ops:
  0.6 31.9 %shard_map.85 = (f32[4,64,128]{2,1,0:T(8,128)S(1)}, f32[4,64,128]{2,1,0:T(8,128)S(1)}, f32[8,128]{1,0:T(8,128)S(1)}) custom-call(f32[4,64,128]{2,1,0:T(8,128)} %probes.1, f32[2,64,128]{2,1,0:T(8,128)} %velocity.1, f32[64,128]{1,0:T(8,128)} %eta_in.1, f32[64,128]{1,0:T(8,128)} %friction.1, f32[64,128]{1,0:T(8,128)} %noise.1, s32[64,128]{1,0:T(8,128)} %ice.1), custom_call_target="tpu_custom_call" | custom-call | tf_op jit(solution)/shard_map/pallas_call | solution.py:633
  32.6 0.9 %shard_map.86 = (f32[4,64,128]{2,1,0:T(8,128)}, f32[4,64,128]{2,1,0:T(8,128)}, f32[8,8]{1,0:T(8,128)}) custom-call(f32[8,128]{1,0:T(8,128)S(1)} %get-tuple-element.6.sums, f32[4,64,128]{2,1,0:T(8,128)S(1)} %get-tuple-element.7.images, f32[4,64,128]{2,1,0:T(8,128)S(1)} %get-tuple-element.8.other_images), custom_call_target="tpu_custom_call" | custom-call | tf_op jit(solution)/shard_map/pallas_call | solution.py:655

commit v5 on v4

--- a/solution.py
+++ b/solution.py
@@ -299,18 +299,20 @@
     unrolled(BI, row)
 
 
-def products(left, left_row, right, right_row):
+def products(lefts, right, right_row):
+    count = 16 * len(lefts)
+
     def add(k, totals):
-        a = [left[p, pl.ds(left_row + 8 * k, 8), :] for p in range(HALF)]
+        a = [left[p, pl.ds(row + 8 * k, 8), :] for left, row in lefts for p in range(HALF)]
         b = [right[p, pl.ds(right_row + 8 * k, 8), :] for p in range(HALF)]
         return tuple(t + a[n // 4] * b[n % 4] for n, t in enumerate(totals))
 
     zero = jnp.zeros((8, 128), F32)
-    totals = lax.fori_loop(0, ROWS // 8, add, (zero,) * 16, unroll=True)
+    totals = lax.fori_loop(0, ROWS // 8, add, (zero,) * count, unroll=True)
     sums = jnp.concatenate([jnp.sum(t, axis=0, keepdims=True) for t in totals], axis=0)
     sums = jnp.sum(sums, axis=1, keepdims=True)
-    lane = lax.broadcasted_iota(jnp.int32, (16, 128), 1)
-    row = lax.broadcasted_iota(jnp.int32, (16, 128), 0)
+    lane = lax.broadcasted_iota(jnp.int32, (count, 128), 1)
+    row = lax.broadcasted_iota(jnp.int32, (count, 128), 0)
     return jnp.sum(jnp.where(lane == row, sums, 0.0), axis=0, keepdims=True)
 
 
@@ -483,18 +485,17 @@
     def _():
         image_copy.start()
 
+
+    @pl.when(half == 0)
+    def _():
+        probe_copy.wait_recv()
+        message[0] = products([(ext, HALO), (other_probes, 0)], natural, HALO)
+
+    @pl.when(half == 1)
+    def _():
+        message[0] = turn(products([(ext, HALO)], natural, HALO), 32, 1)
+
     hear(3)
-    own = products(ext, HALO, natural, HALO)
-
-    @pl.when(half == 0)
-    def _():
-        probe_copy.wait_recv()
-        cross = products(other_probes, 0, natural, HALO)
-        message[0] = own + turn(cross, 16, 1)
-
-    @pl.when(half == 1)
-    def _():
-        message[0] = turn(own, 32, 1)
 
     me = (gx * ny_devices + gy) * 2 + half
     everyone = 2 * nx_devices * ny_devices

time: 33.5 us -> 33.5 us (level)
  no operation moved by 1% of the time
where the time goes in v5:
time: 33.5 us; the launch traced here: 33.4 us
  Pallas kernels  32.8 us (98%)
  between operations  0.64 us (2%)
    pallas_call x1, Pallas kernels, body(): pl.pallas_call(functools.partial(main_kernel, nx_devices, ny_devices), ou...  31.9 us
    pallas_call x1, Pallas kernels, body(): pl.pallas_call(last_kernel, out_shape=(tile, tile, jax.ShapeDtypeStruct(s...  0.87 us

profile of v5, /device:TPU:1, one launch (start us, length us, event | category | flops | bytes accessed | tf_op | source)
XLA Modules:
  0.0 33.4 jit_solution(17395069594908261101)
XLA Ops:
  0.6 31.9 %shard_map.85 = (f32[4,64,128]{2,1,0:T(8,128)S(1)}, f32[4,64,128]{2,1,0:T(8,128)S(1)}, f32[8,128]{1,0:T(8,128)S(1)}) custom-call(f32[4,64,128]{2,1,0:T(8,128)} %probes.1, f32[2,64,128]{2,1,0:T(8,128)} %velocity.1, f32[64,128]{1,0:T(8,128)} %eta_in.1, f32[64,128]{1,0:T(8,128)} %friction.1, f32[64,128]{1,0:T(8,128)} %noise.1, s32[64,128]{1,0:T(8,128)} %ice.1), custom_call_target="tpu_custom_call" | custom-call | tf_op jit(solution)/shard_map/pallas_call | solution.py:634
  32.6 0.9 %shard_map.86 = (f32[4,64,128]{2,1,0:T(8,128)}, f32[4,64,128]{2,1,0:T(8,128)}, f32[8,8]{1,0:T(8,128)}) custom-call(f32[8,128]{1,0:T(8,128)S(1)} %get-tuple-element.6.sums, f32[4,64,128]{2,1,0:T(8,128)S(1)} %get-tuple-element.7.images, f32[4,64,128]{2,1,0:T(8,128)S(1)} %get-tuple-element.8.other_images), custom_call_target="tpu_custom_call" | custom-call | tf_op jit(solution)/shard_map/pallas_call | solution.py:656
